TPU v7x, 768 devices: a whole 4x8x12 slice. The times are simulated.
768 devices in a mesh: tm: 12 (over z), head: 64 (over x, y, core).
Axes of the slice: x: 4, y: 8, z: 12, core: 2. Of those that a mesh axis runs over, the one named last changes fastest.
Arguments:
- xs: bfloat16 [12288, 4096], P('tm', 'head'), may hold values from -6 to 6
- bc: bfloat16 [12288, 256], P('tm'), may hold values from -0.16894531 to 0.16894531
- log_decay: float32 [12288, 64], P('tm', 'head'), may hold values from -1 to 0
- out_grad: bfloat16 [12288, 4096], P('tm', 'head'), may hold values from -6 to 6
- news_owner: int32 [384, 1], P('tm'), may hold values from 0 to 11; in each aligned block of 32 rows (0 to 31, 32 to 63, ...) at most 6 rows name the same one
- news_local: int32 [384, 1], P('tm'), may hold values from 0 to 63
Outputs:
- x_grad: bfloat16 [12288, 4096], P('tm', 'head')
- bc_grad: float32 [12288, 256], P(('tm', 'head'))
- decay_grad: float32 [12288, 64], P('tm', 'head')
- news_grad: float32 [768, 4096], P('tm', 'head')
Inputs may be any that keep to these rules, and one draw needn't show every extreme that they name: `news_owner`: among the groups of events of one index of tm, at most 6 name the same owner; in every draw some owner is named by exactly 6 of one index's groups.
All inputs are finite; a program needn't handle non-finite values.
Results may differ from a plain program's by a relative error of at most 0.0012.
Values sent between devices are 32-bit elements; how exact they have to be, the bound alone decides.
A program may use at most 32 MiB of HBM per device.

v0:
```python
import math

import jax
import jax.numpy as jnp
from jax import lax
from jax.sharding import PartitionSpec as P

NQ = 32
NEWS_DEV = 64


highest = lax.Precision.HIGHEST


def in_one_piece(arrays, axis, dim, along):
    widths = [math.prod(a.shape[along:]) for a in arrays]
    both = jnp.concatenate(
        [a.reshape(*a.shape[:along], w) for a, w in zip(arrays, widths)], axis=along
    )
    out = lax.all_gather(both, axis, axis=dim, tiled=True)
    pieces = jnp.split(out, [sum(widths[:k]) for k in range(1, len(widths))], axis=along)
    return tuple((b.reshape(*out.shape[:along], *a.shape[along:]) for a, b in zip(arrays, pieces)))


def cut_along(x, dim, count):
    dims = x.shape
    pieces = x.reshape(*dims[:dim], count, dims[dim] // count, *dims[dim + 1 :])
    return jnp.moveaxis(pieces, dim, 0)


def sum_at_owner(x, axis, dim):
    count = lax.axis_size(axis)
    pieces = lax.all_to_all(cut_along(x, dim, count), axis, 0, 0, tiled=True)
    return jnp.sum(pieces, axis=0)


def head_grads(x_h, dy_h, x_low, dy_low, cums, start, carry, bmat, cmat, b_low, c_low):
    length = x_h.shape[0]
    index = jnp.arange(length)
    lower = index[:, None] >= index[None, :]
    spread = cums[:, None] - cums[None, :]
    mmat = jnp.where(lower, jnp.exp(jnp.where(lower, spread, 0.0)), 0.0)
    total = cums[-1]
    before = jnp.exp(total - cums)
    after = jnp.exp(cums)
    kxd = jnp.dot(x_low, dy_low.T, preferred_element_type=jnp.float32)
    kcb = jnp.dot(c_low, b_low.T, preferred_element_type=jnp.float32)
    q_mat = mmat * kxd.T
    m_two = mmat * kcb
    b_grad_state = jnp.dot(bmat, carry, precision=highest)
    c_state = jnp.dot(cmat, start, precision=highest)
    dx = jnp.dot(m_two.T, dy_h, precision=highest) + before[:, None] * b_grad_state
    db = jnp.dot(q_mat.T, cmat, precision=highest) + before[:, None] * jnp.dot(
        x_h, carry.T, precision=highest
    )
    dc = after[:, None] * jnp.dot(dy_h, start.T, precision=highest) + jnp.dot(
        q_mat, bmat, precision=highest
    )
    weights = m_two * kxd.T
    row_sums = jnp.cumsum(weights, axis=1)
    inner = jnp.sum(jnp.where(lower, row_sums, 0.0), axis=0)
    zterm = jnp.sum(b_grad_state * x_h, axis=1)
    wterm = jnp.sum(c_state * dy_h, axis=1)
    inner = inner + before * jnp.dot(mmat, zterm, precision=highest)
    inner = inner + after * jnp.dot(mmat.T, wterm, precision=highest)
    inner = inner + jnp.exp(total) * jnp.sum(carry * start)
    dla = inner - jnp.sum(bmat * db, axis=1)
    return (dx, db, dc, dla)


def forward_pass(hcur, item):
    factor, summary = item
    return (factor[:, None, None] * hcur + summary, hcur)


def on_device(xs, bc, log_decay, out_grad, news_owner, news_local):
    length = xs.shape[0]
    heads_local = log_decay.shape[1]
    width = xs.shape[1] // heads_local
    state = bc.shape[1] // 2
    span = min(256, length)
    nblocks = length // span
    inputs_low = xs.reshape(length, heads_local, width).transpose(1, 0, 2)
    grads_low = out_grad.reshape(length, heads_local, width).transpose(1, 0, 2)
    inputs = inputs_low.astype(jnp.float32)
    grads = grads_low.astype(jnp.float32)
    b_low = bc[:, :state]
    c_low = bc[:, state:]
    bmat = b_low.astype(jnp.float32)
    cmat = c_low.astype(jnp.float32)
    log_rows = log_decay.T
    cums_shard = jnp.cumsum(log_rows, axis=1)
    total = cums_shard[:, -1]
    decay = jnp.exp(total)
    log_blocks = log_rows.reshape(heads_local, nblocks, span)
    cums_blocks = jnp.cumsum(log_blocks, axis=2)
    block_total = cums_blocks[:, :, -1]
    before_blocks = jnp.exp(block_total[:, :, None] - cums_blocks)
    after_blocks = jnp.exp(cums_blocks)
    inputs_blocks = inputs.reshape(heads_local, nblocks, span, width)
    grads_blocks = grads.reshape(heads_local, nblocks, span, width)
    b_blocks = bmat.reshape(nblocks, span, state)
    c_blocks = cmat.reshape(nblocks, span, state)
    send_blocks = jnp.einsum(
        "hcl,cln,hclp->hcnp", before_blocks, b_blocks, inputs_blocks, precision=highest
    )
    back_blocks = jnp.einsum(
        "hcl,cln,hclp->hcnp", after_blocks, c_blocks, grads_blocks, precision=highest
    )
    block_decay = jnp.exp(block_total)
    zeros = jnp.zeros((heads_local, state, width), jnp.float32)
    send_state, starts_local = lax.scan(
        forward_pass, zeros, (block_decay.T, send_blocks.transpose(1, 0, 2, 3))
    )
    back_state, carries_local = lax.scan(
        forward_pass, zeros, (block_decay.T, back_blocks.transpose(1, 0, 2, 3)), reverse=True
    )
    all_decay, all_send, all_back = in_one_piece(
        (decay[None], send_state[None], back_state[None]), "tm", 0, 2
    )
    mine = lax.axis_index("tm")
    division_number = lax.axis_size("tm")

    def forward_step(j, hcur):
        return jnp.where(j < mine, all_decay[j][:, None, None] * hcur + all_send[j], hcur)

    def reverse_step(k, gcur):
        j = division_number - 1 - k
        return jnp.where(j > mine, all_decay[j][:, None, None] * gcur + all_back[j], gcur)

    start = lax.fori_loop(0, division_number, forward_step, zeros)
    carry = lax.fori_loop(0, division_number, reverse_step, zeros)
    shard_blocks = cums_shard.reshape(heads_local, nblocks, span)
    prefix = shard_blocks[:, :, 0] - log_blocks[:, :, 0]
    suffix = total[:, None] - shard_blocks[:, :, -1]
    starts = starts_local.transpose(1, 0, 2, 3) + jnp.exp(prefix)[:, :, None, None] * start[:, None]
    carries = (
        carries_local.transpose(1, 0, 2, 3) + jnp.exp(suffix)[:, :, None, None] * carry[:, None]
    )
    per_block = jax.vmap(head_grads, in_axes=(0, 0, 0, 0, 0, 0, 0, 0, 0, 0, 0))
    per_head = jax.vmap(per_block, in_axes=(0, 0, 0, 0, 0, 0, 0, None, None, None, None))
    dx, db, dc, dla = per_head(
        inputs_blocks,
        grads_blocks,
        inputs_low.reshape(heads_local, nblocks, span, width),
        grads_low.reshape(heads_local, nblocks, span, width),
        cums_blocks,
        starts,
        carries,
        b_blocks,
        c_blocks,
        b_low.reshape(nblocks, span, state),
        c_low.reshape(nblocks, span, state),
    )
    dx = dx.reshape(heads_local, length, width)
    db = db.reshape(heads_local, length, state)
    dc = dc.reshape(heads_local, length, state)
    dla = dla.reshape(heads_local, length)
    flat_dx = dx.transpose(1, 0, 2).reshape(length, heads_local * width)
    x_grad = flat_dx.astype(jnp.bfloat16)
    decay_grad = dla.T
    bc_term = jnp.concatenate([db.sum(axis=0), dc.sum(axis=0)], axis=1)
    bc_grad = sum_at_owner(bc_term, "head", 0)
    groups = length // NQ
    group_sums = flat_dx.reshape(groups, NQ, heads_local * width).sum(axis=1)
    owner = news_owner[:, 0]
    local = news_local[:, 0]
    shards_tm = lax.axis_size("tm")
    target = owner * NEWS_DEV + local
    place = (jnp.arange(shards_tm * NEWS_DEV)[:, None] == target[None, :]).astype(jnp.float32)
    outgoing = jnp.dot(place, group_sums, precision=highest).reshape(
        shards_tm, NEWS_DEV, heads_local * width
    )
    incoming = lax.all_to_all(outgoing, "tm", split_axis=0, concat_axis=0, tiled=True)
    news_grad = incoming.sum(axis=0)
    return (x_grad, bc_grad, decay_grad, news_grad)


def solution(mesh):
    placed = (
        P("tm", "head"),
        P("tm", None),
        P("tm", "head"),
        P("tm", "head"),
        P("tm", None),
        P("tm", None),
    )
    return jax.shard_map(
        on_device,
        mesh=mesh,
        in_specs=placed,
        out_specs=(P("tm", "head"), P(("tm", "head"), None), P("tm", "head"), P("tm", "head")),
        check_vma=False,
    )
```

profile of v0, /device:TPU:1, one launch (start us, length us, event | category | flops | bytes accessed | tf_op | source)
XLA Modules:
  0.0 174.0 jit_solution(8668698797898026353)
XLA Ops:
  3.0 1.2 reduce-window.20
  10.3 6.0 %while.60 = (s32[]{:T(128)}, f32[1,128,64]{2,1,0:T(8,128)S(1)}, f32[4,1,128,64]{3,2,1,0:T(8,128)S(1)}, f32[4,1]{0,1:T(1,128)S(1)}, f32[4,1,128,64]{2,3,0,1:T(8,128)S(1)}, /*index=5*/s32[]{:T(128)}, s32[]{:T(128)}, s32[]{:T(128)}) while((s32[]{:T(128)}, f32[1,128,64]{2,1,0:T(8,128)S(1)}, f32[4,1,128,64]{3,2,1,0:T(8,128)S(1)}, ...), condition=%wide.region_3.4_spmd.clone, body=%wide.region_2.3_spmd.clone.sunk | while | flops 32772 | bytes 360588 | solution.py:115
  16.7 5.6 %while.61 = (s32[]{:T(128)}, f32[1,128,64]{2,1,0:T(8,128)S(1)}, f32[4,1,128,64]{3,2,1,0:T(8,128)S(1)}, f32[4,1]{0,1:T(1,128)S(1)}, f32[4,1,128,64]{2,3,0,1:T(8,128)S(1)}, /*index=5*/s32[]{:T(128)}, s32[]{:T(128)}) while((s32[]{:T(128)}, f32[1,128,64]{2,1,0:T(8,128)S(1)}, f32[4,1,128,64]{3,2,1,0:T(8,128)S(1)}, ...), condition=%wide.region_7.8_spmd.clone, body=%wide.region_6.7_spmd.clone.sunk | while | flops 32771 | bytes 360568 | solution.py:112
  22.7 32.7 %all_gather.3 = f32[12,1,16385]{2,1,0:T(1,128)S(1)} all-gather(f32[1,1,16385]{2,1,0:T(1,128)S(1)} %concatenate.11), channel_id=1, replica_groups=mesh['tm'=12,'head'=64] {'tm'}, dimensions={0}, use_global_device_ids=true | all-gather | bytes 852020 | tf_op jit(solution)/shard_map/all_gather | solution.py:20
  56.1 2.7 %slice_reduce_fusion = (f32[12,8192]{1,0:T(8,128)}, f32[12,8192]{1,0:T(8,128)S(1)}) fusion(f32[12,1,16385]{2,1,0:T(1,128)S(1)} %all_gather.3), kind=kLoop, calls=%fused_computation.57 | loop fusion | bytes 1572864 | tf_op jit(solution)/shard_map/split | solution.py:21
  61.0 21.4 %while.62 = (s32[]{:T(128)}, f32[1,128,64]{2,1,0:T(8,128)S(1)}, s32[]{:T(128)}, f32[12,1]{0,1:T(1,128)}, f32[12,1,128,64]{3,2,1,0:T(8,128)S(1)}, /*index=5*/s32[]{:T(128)}, s32[]{:T(128)}, s32[]{:T(128)}, s32[]{:T(128)}) while((s32[]{:T(128)}, f32[1,128,64]{2,1,0:T(8,128)S(1)}, s32[]{:T(128)}, f32[12,1]{0,1:T(1,128)}, ...), condition=%wide.region_9.10_spmd.clone, body=%wide.region_8.9_spmd.clone.sunk | while | flops 32776 | bytes 98491 | solution.py:132
  61.0 1.2 constant_dynamic-slice_fusion.16
  62.8 1.2 constant_dynamic-slice_fusion.16
  64.6 1.2 constant_dynamic-slice_fusion.16
  89.0 4.2 %all-to-all-start.1 = ((f32[12,1,4096]{2,1,0:T(1,128)}), f32[12,1,4096]{2,1,0:T(1,128)}, u32[]{:S(2)}, u32[]{:S(2)}) async-start(f32[12,1,4096]{2,1,0:T(1,128)} %reshape.605), calls=%async_computation.1 | async-start | bytes 393216 | tf_op jit(solution)/shard_map/all_to_all | solution.py:174
  93.2 1.3 fusion.3
  94.6 1.3 bitcast_multiply_fusion
  95.9 1.4 reshape.580
  97.3 22.5 %while.63 = (s32[]{:T(128)}, f32[1,128,64]{2,1,0:T(8,128)S(1)}, s32[]{:T(128)}, f32[12,1]{0,1:T(1,128)}, f32[12,1,128,64]{3,2,1,0:T(8,128)S(1)}, /*index=5*/s32[]{:T(128)}, s32[]{:T(128)}) while((s32[]{:T(128)}, f32[1,128,64]{2,1,0:T(8,128)S(1)}, s32[]{:T(128)}, f32[12,1]{0,1:T(1,128)}, f32[12,1,128,64]{3,2,1,0:T(8,128)S(1)}, ...), condition=%wide.region_11.12_spmd.clone, body=%wide.region_10.11_spmd.clone.sunk | while | flops 32772 | bytes 98429 | solution.py:131
  97.3 1.2 constant_dynamic-slice_fusion.17
  99.2 1.2 constant_dynamic-slice_fusion.17
  101.1 1.2 constant_dynamic-slice_fusion.17
  103.0 1.2 constant_dynamic-slice_fusion.17
  104.8 1.2 constant_dynamic-slice_fusion.17
  106.7 1.2 constant_dynamic-slice_fusion.17
  108.6 1.2 constant_dynamic-slice_fusion.17
  110.4 1.2 constant_dynamic-slice_fusion.17
  112.3 1.2 constant_dynamic-slice_fusion.17
  114.2 1.2 constant_dynamic-slice_fusion.17
  116.1 1.2 constant_dynamic-slice_fusion.17
  117.9 1.2 constant_dynamic-slice_fusion.17
  119.8 3.7 %multiply_reduce_fusion = (f32[4,256]{1,0:T(4,128)}, f32[4,256,128]{2,1,0:T(8,128)}) fusion(bf16[4,256,128]{2,1,0:T(8,128)(2,1)S(1)} %bitcast.230, f32[4,256,128]{2,1,0:T(8,128)} %fusion.3, bf16[4,256,128]{2,1,0:T(8,128)(2,1)S(1)} %bitcast.234, f32[1,4,256,256]{2,3,1,0:T(8,128)} %get-tuple-element.553, f32[4,256]{1,0:T(4,128)S(1)} %get-tuple-element.545, ...), kind=kOutput, calls=%fused_computation.40 | convolution fusion | flops 404225024 | bytes 2695168 | tf_op jit(solution)/shard_map/vmap(vmap())/dot_general | solution.py:53
  125.7 2.1 %pad_maximum_fusion = f32[64,16,256]{2,1,0:T(8,128)} fusion(f32[64,16,128]{2,1,0:T(8,128)S(1)} %bitcast.237, f32[64,16,128]{2,1,0:T(8,128)} %bitcast.242), kind=kLoop, calls=%fused_computation.29 | loop fusion | flops 262144 | bytes 2097152 | tf_op jit(solution)/shard_map/concatenate | solution.py:162
  128.7 16.1 %all-to-all-start = ((f32[64,16,256]{2,1,0:T(8,128)}), f32[64,16,256]{2,1,0:T(8,128)S(1)}, u32[]{:S(2)}, u32[]{:S(2)}) async-start(f32[64,16,256]{2,1,0:T(8,128)} %pad_maximum_fusion), calls=%async_computation | async-start | bytes 2097152 | tf_op jit(solution)/shard_map/all_to_all | solution.py:33
  149.3 1.2 fusion.10
  152.7 2.0 %reduce.25 = f32[12,4096]{1,0:T(8,128)S(1)} reduce(f32[12,1,4096]{2,1,0:T(1,128)} %all-to-all-done.1, f32[]{:T(128)} %broadcast.274), dimensions={1}, to_apply=%all_to_all.7.reduce_sub_computation | reduce | bytes 393220 | tf_op jit(solution)/shard_map/all_to_all | solution.py:174
  155.6 17.8 %all-to-all-done = f32[64,16,256]{2,1,0:T(8,128)S(1)} async-done(((f32[64,16,256]{2,1,0:T(8,128)}), f32[64,16,256]{2,1,0:T(8,128)S(1)}, u32[]{:S(2)}, u32[]{:S(2)}) %all-to-all-start) | async-done | bytes 1048608 | tf_op jit(solution)/shard_map/all_to_all | solution.py:33
  (188 shorter events, 65.0 us)
Async XLA Ops:
  0.6 0.7 copy-start.9
  8.2 0.5 copy-start.17
  8.8 1.1 copy-start
  9.9 72.4 %copy-start.1 = (bf16[1024,128]{1,0:T(8,128)(2,1)}, bf16[1024,128]{1,0:T(8,128)(2,1)S(1)}, u32[]{:S(2)}) copy-start(bf16[1024,128]{1,0:T(8,128)(2,1)S(1)} %get-tuple-element.549) | copy-start | bytes 786436
  10.3 6.2 %copy-start.4 = (bf16[1024,64]{0,1:T(8,128)(2,1)S(1)}, bf16[1024,64]{0,1:T(8,128)(2,1)}, u32[]{:S(2)}) copy-start(bf16[1024,64]{0,1:T(8,128)(2,1)} %param.14) | copy-start | bytes 393220
  61.0 21.4 %copy-start.6 = (pred[256,256]{0,1:T(8,128)(4,1)S(1)}, pred[256,256]{0,1:T(8,128)(4,1)}, u32[]{:S(2)}) copy-start(pred[256,256]{0,1:T(8,128)(4,1)} %iota_compare_fusion.1) | copy-start | bytes 196612
  82.4 0.7 copy-start.11
  83.1 0.7 copy-start.12
  86.2 0.7 copy-start.19
  86.2 0.7 copy-start.20
  86.9 0.7 copy-start.10
  89.0 39.7 %all-to-all-start.1 = ((f32[12,1,4096]{2,1,0:T(1,128)}), f32[12,1,4096]{2,1,0:T(1,128)}, u32[]{:S(2)}, u32[]{:S(2)}) async-start(f32[12,1,4096]{2,1,0:T(1,128)} %reshape.605), calls=%async_computation.1 | async-start | bytes 393216 | tf_op jit(solution)/shard_map/all_to_all | solution.py:174
  95.9 23.9 %copy-start.2 = (bf16[1024,128]{1,0:T(8,128)(2,1)S(1)}, bf16[1024,128]{1,0:T(8,128)(2,1)}, u32[]{:S(2)}) copy-start(bf16[1024,128]{1,0:T(8,128)(2,1)} %copy-done.1) | copy-start | bytes 786436
  97.3 22.5 %copy-start.7 = (pred[256,256]{0,1:T(8,128)(4,1)S(1)}, pred[256,256]{0,1:T(8,128)(4,1)}, u32[]{:S(2)}) copy-start(pred[256,256]{0,1:T(8,128)(4,1)} %iota_compare_fusion.1) | copy-start | bytes 196612
  119.8 4.8 %copy-start.5 = (f32[1,4,256,256]{2,3,1,0:T(8,128)S(1)}, f32[1,4,256,256]{2,3,1,0:T(8,128)}, u32[]{:S(2)}) copy-start(f32[1,4,256,256]{2,3,1,0:T(8,128)} %get-tuple-element.553) | copy-start | bytes 3145732
  123.6 0.7 copy-start.13
  128.7 44.6 %all-to-all-start = ((f32[64,16,256]{2,1,0:T(8,128)}), f32[64,16,256]{2,1,0:T(8,128)S(1)}, u32[]{:S(2)}, u32[]{:S(2)}) async-start(f32[64,16,256]{2,1,0:T(8,128)} %pad_maximum_fusion), calls=%async_computation | async-start | bytes 2097152 | tf_op jit(solution)/shard_map/all_to_all | solution.py:33
  146.9 0.7 copy-start.14
  147.5 0.9 copy-start.3
  148.5 0.6 copy-start.18
  148.5 0.8 copy-start.8
  149.3 1.3 copy-start.15
  150.6 1.0 copy-start.16
where the time goes:
time: 175 us; the launch traced here: 174 us
  local copies, waits for them, and re-layouts  53.4 us (31%)
  other arithmetic  32.8 us (19%)
  blocking collectives  32.7 us (19%)
  starting transfers between devices  20.2 us (12%)
  waiting for transfers between devices  17.8 us (10%)
  matrix products  13.7 us (8%)
  between operations  2.36 us (1%)
    all_gather x1, blocking collectives, in_one_piece(): out = lax.all_gather(both, axis, axis=dim, tiled=True)  32.7 us
    all_to_all x1, waiting for transfers between devices, sum_at_owner(): pieces = lax.all_to_all(cut_along(x, dim, count), axis, 0, 0, tiled=True)  17.8 us
    all_to_all x1, starting transfers between devices, sum_at_owner(): pieces = lax.all_to_all(cut_along(x, dim, count), axis, 0, 0, tiled=True)  16.1 us
    dynamic_slice x12, local copies, waits for them, and re-layouts, forward_step(): all_decay[j][:, None, None] * hcur + all_send[j]  14.2 us
    dynamic_slice x12, local copies, waits for them, and re-layouts, reverse_step(): all_decay[j][:, None, None] * gcur + all_back[j]  14.1 us
    select_n x12, other arithmetic, forward_step(): jnp.where(j < mine, all_decay[j][:, None, None] * hcur + all_send[j], hcur)  7.91 us
    unnamed x47, local copies, waits for them, and re-layouts  7.82 us
    select_n x12, other arithmetic, reverse_step(): jnp.where(j > mine, all_decay[j][:, None, None] * gcur + all_back[j], gcur)  6.87 us
  transfers between devices with their start and end apart: 2, of which 1 were waited for; matrix products, arithmetic and copies ran while one was open for 25% of the time, Pallas kernels for 0%

commit v1 on v0

v1 whole, which is shorter than its diff:
```python
import functools

import jax
import jax.numpy as jnp
from jax import lax
from jax.experimental import pallas as pl
from jax.experimental.pallas import tpu as pltpu
from jax.sharding import PartitionSpec as P

MESH = pl.DeviceIdType.MESH
F32 = jnp.float32
BF16 = jnp.bfloat16
NEWS_DEV = 64
NQ = 32
L = 128


def nn(a, b):
    return lax.dot_general(a, b, (((1,), (0,)), ((), ())), preferred_element_type=F32)


def nt(a, b):
    return lax.dot_general(a, b, (((1,), (1,)), ((), ())), preferred_element_type=F32)


def split2(v):
    hi = v.astype(BF16)
    return hi, (v - hi.astype(F32)).astype(BF16)


def split3(v):
    one = v.astype(BF16).astype(F32)
    two = (v - one).astype(BF16).astype(F32)
    return one, two, v - one - two


def iota(shape, dim):
    return lax.broadcasted_iota(jnp.int32, shape, dim)


class Plan:
    def __init__(self, tm, x, y, slots):
        self.tm, self.x, self.y, self.slots = tm, x, y, slots
        self.thirds = tm % 3 == 0
        self.owners = tm // 3 * 2 if self.thirds else tm
        self.rows = 64 // self.owners
        self.block = 1024 // (x * y * 2)
        self.blocks = L // (2 * self.block)

    def is_owner(self, z):
        return lax.rem(z, 3) != 2 if self.thirds else z >= 0

    def owner(self, z):
        return (z // 3) * 2 + lax.rem(z, 3) if self.thirds else z

    def owner_z(self, q):
        return (q // 2) * 3 + q % 2 if self.thirds else q


def kernel(
    plan,
    x_hbm, dy_hbm, bc_hbm, la_hbm, own_hbm, loc_hbm,
    xg_ref, bcg_ref, dla_ref, news_ref,
    xv, dyv, bcv, lav, ownv, locv,
    xd, dyd, acol, bcol, st_loc, ca_loc, pre_b, suf_b, rows_v,
    loc_bc, dbc, crecv, csum, xr1, xr2, ysum, yrecv,
    y_loc, dx_loc, st2, ca2, place_v, ids_v, ve,
    dec_s, dec_r, zs, zr, zo, zb, ns, nr,
    in_sem, dec_ss, dec_rs, z1_ss, z1_rs, z2_ss, z2_rs,
    c_ss, c_rs, x1_ss, x1_rs, x2_ss, x2_rs, y_ss, y_rs, n_ss, n_rs,
):
    nz, ny, nx = plan.tm, plan.y, plan.x
    zi = lax.axis_index("tm")
    hi_ = lax.axis_index("head")
    core = lax.rem(hi_, 2)
    yi = lax.rem(hi_ // 2, ny)
    xi = hi_ // (2 * ny)

    def head(x, y, c):
        return (x * ny + y) * 2 + c

    def at_z(z):
        return (z, hi_)

    def at_head(h):
        return (zi, h)

    right = at_head(head(lax.rem(xi + 1, nx), yi, core))
    left = at_head(head(lax.rem(xi + nx - 1, nx), yi, core))
    twin = at_head(head(xi, yi, 1 - core))

    loads = [
        pltpu.make_async_copy(src, dst, in_sem.at[k])
        for k, (src, dst) in enumerate(
            ((la_hbm, lav), (x_hbm, xv), (bc_hbm, bcv), (dy_hbm, dyv), (own_hbm, ownv), (loc_hbm, locv))
        )
    ]
    for load in loads:
        load.start()

    barrier = pltpu.get_barrier_semaphore()
    greeted = [at_z(lax.rem(zi + d, nz)) for d in range(1, nz)]
    greeted += [twin, left, right]
    greeted += [at_head(head(xi, lax.rem(yi + d, ny), core)) for d in range(1, ny)]
    for device in greeted:
        pl.semaphore_signal(barrier, inc=1, device_id=device, device_id_type=MESH)

    up = jnp.where(iota((L, L), 0) <= iota((L, L), 1), 1.0, 0.0).astype(BF16)
    down = jnp.where(iota((L, L), 0) >= iota((L, L), 1), 1.0, 0.0).astype(BF16)
    loads[0].wait()
    parts = split3(lav[...])
    sums = nn(jnp.concatenate([*parts, jnp.zeros((8, L), F32)], axis=0).astype(BF16), up)
    cums = sums[0:8] + sums[8:16] + sums[16:24]
    tot = jnp.broadcast_to(cums[:, L - 1 : L], (8, L))
    after = jnp.exp(cums)
    before = jnp.exp(tot - cums)
    chunk_decay = jnp.exp(tot)
    tots = [tot[c : c + 1] for c in range(8)]
    run = jnp.zeros((1, L), F32)
    for c in range(8):
        pre_b[c] = jnp.broadcast_to(jnp.exp(run), (8, L))
        run = run + tots[c]
    device_decay = jnp.exp(run)
    run = jnp.zeros((1, L), F32)
    for c in reversed(range(8)):
        suf_b[c] = jnp.broadcast_to(jnp.exp(run), (8, L))
        run = run + tots[c]
    dec_s[...] = device_decay
    dec_r[zi] = device_decay

    pl.semaphore_wait(barrier, len(greeted))

    def dec_copy(d):
        to = lax.rem(zi + d, nz)
        return to, pltpu.make_async_remote_copy(
            src_ref=dec_s, dst_ref=dec_r.at[zi], send_sem=dec_ss.at[d], recv_sem=dec_rs.at[zi],
            device_id=at_z(to), device_id_type=MESH,
        )

    for d in range(1, nz):
        to, copy = dec_copy(d)
        pl.when(plan.is_owner(to))(copy.start)

    loads[1].wait()
    loads[2].wait()
    state = jnp.zeros((64, L), F32)
    for c in range(8):
        part = slice(c * L, (c + 1) * L)
        hi, lo = split2(xv[:, part].astype(F32) * before[c : c + 1])
        bm = bcv[part, 0:L]
        st_loc[c] = state
        state = state * chunk_decay[c : c + 1] + nn(
            jnp.concatenate([hi, lo], axis=1), jnp.concatenate([bm, bm], axis=0)
        )
    st_loc[8] = state
    loads[3].wait()
    back = jnp.zeros((64, L), F32)
    for c in reversed(range(8)):
        part = slice(c * L, (c + 1) * L)
        hi, lo = split2(dyv[:, part].astype(F32) * after[c : c + 1])
        cm = bcv[part, L : 2 * L]
        ca_loc[c] = back
        back = back * chunk_decay[c : c + 1] + nn(
            jnp.concatenate([hi, lo], axis=1), jnp.concatenate([cm, cm], axis=0)
        )
    zs[:, 0] = state.reshape(plan.owners, plan.rows, L)
    zs[:, 1] = back.reshape(plan.owners, plan.rows, L)

    def z1_copy(d):
        to = lax.rem(zi + d, nz)
        return to, pltpu.make_async_remote_copy(
            src_ref=zs.at[plan.owner(to)], dst_ref=zr.at[zi], send_sem=z1_ss.at[d], recv_sem=z1_rs.at[zi],
            device_id=at_z(to), device_id_type=MESH,
        )

    for d in range(1, nz):
        to, copy = z1_copy(d)

        @pl.when(plan.is_owner(to))
        def _():
            copy.start()

    big = jnp.concatenate([cums, after, before, jnp.zeros((L - 24, L), F32)], axis=0).T
    lower = iota((L, L), 0) >= iota((L, L), 1)
    upper = iota((L, L), 0) <= iota((L, L), 1)
    rows_v[0] = after
    rows_v[1] = before

    def local(c):
        part = slice(c * L, (c + 1) * L)
        bm, cm = bcv[part, 0:L], bcv[part, L : 2 * L]
        xt, dyt = xv[:, part], dyv[:, part]
        xf, dyf = xt.astype(F32), dyt.astype(F32)
        x2 = jnp.concatenate([xf, xf], axis=0).T.astype(BF16)
        dy2 = jnp.concatenate([dyf, dyf], axis=0).T.astype(BF16)
        xd[c] = x2
        dyd[c] = dy2
        col = jnp.broadcast_to(big[:, c : c + 1], (L, L))
        acol[c] = jnp.broadcast_to(big[:, 8 + c : 9 + c], (L, L))
        bcol[c] = jnp.broadcast_to(big[:, 16 + c : 17 + c], (L, L))
        row = jnp.broadcast_to(cums[c : c + 1], (L, L))
        m = jnp.exp(jnp.where(lower, col - row, -1e30))
        mt = jnp.exp(jnp.where(upper, row - col, -1e30))
        w = split2(m * nt(cm, bm))
        q = split2(m * nn(dy2[:, 0:64], xt))
        qt = split2(mt * nn(x2[:, 0:64], dyt))
        loc_bc[c, :, 0:L] = nn(jnp.concatenate(qt, axis=1), jnp.concatenate([cm, cm], axis=0))
        loc_bc[c, :, L : 2 * L] = nn(jnp.concatenate(q, axis=1), jnp.concatenate([bm, bm], axis=0))
        y_loc[c] = nt(jnp.concatenate([xt, xt], axis=1), jnp.concatenate(w, axis=1))
        dx_loc[c] = nn(jnp.concatenate([dyt, dyt], axis=1), jnp.concatenate(w, axis=0))

    for c in range(4):
        local(c)

    @pl.when(plan.is_owner(zi))
    def _():
        zr[zi] = zs[plan.owner(zi)]
        for d in range(1, nz):
            source = lax.rem(zi + nz - d, nz)
            pltpu.make_async_remote_copy(
                src_ref=dec_s, dst_ref=dec_r.at[source], send_sem=dec_ss.at[d], recv_sem=dec_rs.at[source],
                device_id=at_z(source), device_id_type=MESH,
            ).wait_recv()
            pltpu.make_async_remote_copy(
                src_ref=zs.at[0], dst_ref=zr.at[source], send_sem=z1_ss.at[d], recv_sem=z1_rs.at[source],
                device_id=at_z(source), device_id_type=MESH,
            ).wait_recv()
        run = jnp.zeros((plan.rows, L), F32)
        for j in range(nz):
            zo[j, 0] = run
            run = run * dec_r[j] + zr[j, 0]
        run = jnp.zeros((plan.rows, L), F32)
        for j in reversed(range(nz)):
            zo[j, 1] = run
            run = run * dec_r[j] + zr[j, 1]
        mine = plan.owner(zi)
        for d in range(1, nz):
            to = lax.rem(zi + d, nz)
            pltpu.make_async_remote_copy(
                src_ref=zo.at[to], dst_ref=zb.at[mine], send_sem=z2_ss.at[d], recv_sem=z2_rs.at[mine],
                device_id=at_z(to), device_id_type=MESH,
            ).start()
        zb[mine] = zo[zi]

    for c in range(4, 8):
        local(c)
    ns_rows = nz * plan.slots
    loads[4].wait()
    loads[5].wait()
    owner_row = ownv[...]
    named = jnp.where(iota((16, NQ), 0) == owner_row, 1.0, 0.0)
    earlier = jnp.where(iota((NQ, NQ), 0) < iota((NQ, NQ), 1), 1.0, 0.0)
    rank = jnp.sum(named * nn(named.astype(BF16), earlier.astype(BF16)), axis=0, keepdims=True)
    slot = owner_row.astype(F32) * plan.slots + rank
    spread = jnp.where(iota((NQ, 1024), 0) == iota((NQ, 1024), 1) // NQ, 1.0, 0.0).astype(BF16)
    slot_t = nn(jnp.broadcast_to(slot, (16, NQ)).astype(BF16), spread)
    for c in range(8):
        hit = slot_t[0:1, c * L : (c + 1) * L] == iota((ns_rows, L), 0).astype(F32)
        place_v[c] = jnp.where(hit, 1.0, 0.0).astype(BF16)
    hit = slot == iota((ns_rows, NQ), 0).astype(F32)
    ids = jnp.sum(jnp.where(hit, locv[...].astype(F32) + 1.0, 0.0), axis=1, keepdims=True)
    ids_v[...] = jnp.where(iota((ns_rows, L), 1) >= 64, ids, 0.0)

    for q in range(plan.owners):
        source = plan.owner_z(q)

        @pl.when(source != zi)
        def _():
            pltpu.make_async_remote_copy(
                src_ref=zo.at[0], dst_ref=zb.at[q], send_sem=z2_ss.at[0], recv_sem=z2_rs.at[q],
                device_id=at_z(source), device_id_type=MESH,
            ).wait_recv()

    start = zb[:, 0].reshape(64, L)
    carry = zb[:, 1].reshape(64, L)

    def with_edge(local_state, scale, edge):
        return local_state + (edge.reshape(8, 8, L) * scale[None]).reshape(64, L)

    def core_copy(c, k):
        return pltpu.make_async_remote_copy(
            src_ref=dbc.at[c, :, 1 - core], dst_ref=crecv.at[c], send_sem=c_ss.at[k], recv_sem=c_rs.at[k],
            device_id=twin, device_id_type=MESH,
        )

    def finish_bc(c, k):
        st = jnp.concatenate(split2(with_edge(st_loc[c], pre_b[c], start)), axis=0)
        ca = jnp.concatenate(split2(with_edge(ca_loc[c], suf_b[c], carry)), axis=0)
        st2[c] = st
        ca2[c] = ca
        shape = (plan.blocks, 2, plan.block, L)
        dbc[c, :, :, :, 0:L] = (loc_bc[c, :, 0:L] + bcol[c] * nn(xd[c], ca)).reshape(shape)
        dbc[c, :, :, :, L : 2 * L] = (loc_bc[c, :, L : 2 * L] + acol[c] * nn(dyd[c], st)).reshape(shape)
        core_copy(c, k).start()

    far = lax.rem(xi + 2, nx)
    east = lax.rem(xi + 1, nx)
    west = lax.rem(xi + nx - 1, nx)
    order = [2 * far, 2 * far + 1, 2 * east + 1, 2 * west, 2 * east, 2 * west + 1, 2 * xi, 2 * xi + 1]
    for k, c in enumerate(order):
        finish_bc(c, k)

    def core_sum(k):
        c = order[k]
        core_copy(c, k).wait_recv()
        csum[k] = dbc[c, :, core] + crecv[c]

    def x_copy(k, dst, sems, r, device):
        return pltpu.make_async_remote_copy(
            src_ref=csum.at[k], dst_ref=dst.at[r], send_sem=sems[0].at[r], recv_sem=sems[1].at[r],
            device_id=device, device_id_type=MESH,
        )

    x1 = [x_copy(0, xr1, (x1_ss, x1_rs), 0, right), x_copy(1, xr1, (x1_ss, x1_rs), 1, left)]
    x2 = [
        x_copy(2, xr2, (x2_ss, x2_rs), 0, right),
        x_copy(3, xr2, (x2_ss, x2_rs), 1, left),
        x_copy(4, xr2, (x2_ss, x2_rs), 2, right),
        x_copy(5, xr2, (x2_ss, x2_rs), 3, left),
    ]
    for k in range(2):
        core_sum(k)
        x1[k].start()
    for k in range(2, 4):
        core_sum(k)
        x2[k - 2].start()
    for k in range(4, 8):
        core_sum(k)

    def finish_dx(c, acc):
        part = slice(c * L, (c + 1) * L)
        bm, cm = bcv[part, 0:L], bcv[part, L : 2 * L]
        ys = nt(st2[c], cm)
        dxs = nt(ca2[c], bm)
        yt = y_loc[c] + rows_v[0, c : c + 1] * (ys[0:64] + ys[64:128])
        dxt = dx_loc[c] + rows_v[1, c : c + 1] * (dxs[0:64] + dxs[64:128])
        hi, lo = split2(dxt)
        xg_ref[:, part] = hi
        none = jnp.zeros((64, L), BF16)
        both = jnp.concatenate(
            [jnp.concatenate([hi, none], axis=0), jnp.concatenate([lo, none], axis=0)], axis=1
        )
        place = place_v[c]
        v = jnp.sum(dyv[:, part].astype(F32) * yt - xv[:, part].astype(F32) * dxt, axis=0, keepdims=True)
        if c < 7:
            end = with_edge(st_loc[c + 1], pre_b[c + 1], start)
        else:
            end = with_edge(st_loc[8], jnp.broadcast_to(device_decay, (8, L)), start)
        edge = jnp.sum(with_edge(ca_loc[c], suf_b[c], carry) * end, axis=0, keepdims=True)
        ve[c : c + 1, 0:L] = v
        ve[c : c + 1, L : 2 * L] = edge
        return acc + nt(jnp.concatenate([place, place], axis=1), both)

    acc = ids_v[...]
    for c in range(4):
        acc = finish_dx(c, acc)
    for k in range(2):
        x1[k].wait_recv()
        csum[4 + k] = csum[4 + k] + xr1[k]
        x2[2 + k].start()
    for c in range(4, 8):
        acc = finish_dx(c, acc)
    ns[...] = acc.reshape(nz, plan.slots, L)

    def news_copy(d):
        to = lax.rem(zi + d, nz)
        return pltpu.make_async_remote_copy(
            src_ref=ns.at[to], dst_ref=nr.at[zi], send_sem=n_ss.at[d], recv_sem=n_rs.at[zi],
            device_id=at_z(to), device_id_type=MESH,
        )

    for d in range(1, nz):
        news_copy(d).start()
    nr[zi] = ns[zi]

    parts = [p for p in split3(ve[...])]
    sums = nn(
        jnp.concatenate([*parts, jnp.zeros((8, 2 * L), F32)], axis=0).astype(BF16),
        jnp.concatenate([down, jnp.ones((L, L), BF16)], axis=0),
    )
    dla_ref[...] = sums[0:8] + sums[8:16] + sums[16:24]

    def y_copy(d):
        to = lax.rem(yi + d, ny)
        return pltpu.make_async_remote_copy(
            src_ref=ysum.at[to], dst_ref=yrecv.at[yi], send_sem=y_ss.at[d], recv_sem=y_rs.at[yi],
            device_id=at_head(head(xi, to, core)), device_id_type=MESH,
        )

    for k in range(4):
        x2[k].wait_recv()
    ysum[0 : plan.blocks] = csum[6] + xr2[2] + xr2[1]
    ysum[plan.blocks : 2 * plan.blocks] = csum[7] + xr2[0] + xr2[3]
    for d in range(1, ny):
        y_copy(d).start()
    total = ysum[yi]

    for d in range(1, nz):
        source = lax.rem(zi + nz - d, nz)
        pltpu.make_async_remote_copy(
            src_ref=ns.at[0], dst_ref=nr.at[source], send_sem=n_ss.at[d], recv_sem=n_rs.at[source],
            device_id=at_z(source), device_id_type=MESH,
        ).wait_recv()
    tiles = nr[...].reshape(ns_rows, L)
    lane = iota((ns_rows, L), 1)
    row_hit = jnp.where((lane >= 64) & (tiles == (lane - 63).astype(F32)), 1.0, 0.0).T.astype(BF16)
    hi, lo = split2(tiles)
    news_ref[...] = (nn(row_hit, hi) + nn(row_hit, lo))[64:128, 0:64]

    for d in range(1, ny):
        source = lax.rem(yi + ny - d, ny)
        pltpu.make_async_remote_copy(
            src_ref=ysum.at[0], dst_ref=yrecv.at[source], send_sem=y_ss.at[d], recv_sem=y_rs.at[source],
            device_id=twin, device_id_type=MESH,
        ).wait_recv()
        total = total + yrecv[source]
    bcg_ref[...] = total

    for d in range(1, nz):
        to, copy = dec_copy(d)
        pl.when(plan.is_owner(to))(copy.wait_send)
        to, copy = z1_copy(d)

        @pl.when(plan.is_owner(to))
        def _():
            copy.wait_send()

        news_copy(d).wait_send()

    @pl.when(plan.is_owner(zi))
    def _():
        for d in range(1, nz):
            pltpu.make_async_remote_copy(
                src_ref=zo.at[0], dst_ref=zb.at[0], send_sem=z2_ss.at[d], recv_sem=z2_rs.at[0],
                device_id=at_z(lax.rem(zi + d, nz)), device_id_type=MESH,
            ).wait_send()

    for k, c in enumerate(order):
        core_copy(c, k).wait_send()
    for copy in x1 + x2:
        copy.wait_send()
    for d in range(1, ny):
        y_copy(d).wait_send()


def on_device(plan, xs, bc, log_decay, out_grad, news_owner, news_local):
    rows = plan.tm * plan.slots
    dma = pltpu.SemaphoreType.DMA
    vm = pltpu.VMEM
    slab = (plan.blocks, plan.block, 2 * L)
    scratch = [
        vm((64, 1024), BF16), vm((64, 1024), BF16), vm((1024, 2 * L), BF16), vm((8, L), F32),
        vm((1, NQ), jnp.int32), vm((1, NQ), jnp.int32),
        vm((8, L, L), BF16), vm((8, L, L), BF16), vm((8, L, L), F32), vm((8, L, L), F32),
        vm((9, 64, L), F32), vm((8, 64, L), F32), vm((8, 8, L), F32), vm((8, 8, L), F32), vm((2, 8, L), F32),
        vm((8, L, 2 * L), F32), vm((8, plan.blocks, 2, plan.block, 2 * L), F32),
        vm((8, *slab), F32), vm((8, *slab), F32), vm((2, *slab), F32), vm((4, *slab), F32),
        vm((plan.y, plan.block, 2 * L), F32), vm((plan.y, plan.block, 2 * L), F32),
        vm((8, 64, L), F32), vm((8, 64, L), F32), vm((8, L, L), BF16), vm((8, L, L), BF16),
        vm((8, rows, L), BF16), vm((rows, L), F32), vm((8, 2 * L), F32),
        vm((1, L), F32), vm((plan.tm, 1, L), F32),
        vm((plan.owners, 2, plan.rows, L), F32), vm((plan.tm, 2, plan.rows, L), F32),
        vm((plan.tm, 2, plan.rows, L), F32), vm((plan.owners, 2, plan.rows, L), F32),
        vm((plan.tm, plan.slots, L), F32), vm((plan.tm, plan.slots, L), F32),
        dma((6,)),
        dma((plan.tm,)), dma((plan.tm,)), dma((plan.tm,)), dma((plan.tm,)), dma((plan.tm,)), dma((plan.tm,)),
        dma((8,)), dma((8,)), dma((2,)), dma((2,)), dma((4,)), dma((4,)),
        dma((plan.y,)), dma((plan.y,)), dma((plan.tm,)), dma((plan.tm,)),
    ]
    vmem = pl.BlockSpec(memory_space=pltpu.VMEM)
    anywhere = pl.BlockSpec(memory_space=pl.ANY)
    xg, bcg, dla, news = pl.pallas_call(
        functools.partial(kernel, plan),
        out_shape=(
            jax.ShapeDtypeStruct((64, 1024), BF16),
            jax.ShapeDtypeStruct((plan.block, 2 * L), F32),
            jax.ShapeDtypeStruct((8, L), F32),
            jax.ShapeDtypeStruct((NEWS_DEV, 64), F32),
        ),
        in_specs=[anywhere] * 6,
        out_specs=(vmem,) * 4,
        scratch_shapes=scratch,
        compiler_params=pltpu.CompilerParams(
            collective_id=0, has_side_effects=True, vmem_limit_bytes=40 * 2**20
        ),
    )(
        xs.T, out_grad.T, bc, log_decay.reshape(8, L), news_owner.reshape(1, NQ), news_local.reshape(1, NQ)
    )
    return xg.T, bcg, dla.reshape(1024, 1), news


def solution(mesh):
    tm, heads = mesh.shape["tm"], mesh.shape["head"]
    plan = Plan(tm, 4, heads // 8, 8 if tm == 12 else 32)
    return jax.shard_map(
        functools.partial(on_device, plan),
        mesh=mesh,
        in_specs=(
            P("tm", "head"), P("tm", None), P("tm", "head"), P("tm", "head"), P("tm", None), P("tm", None),
        ),
        out_specs=(P("tm", "head"), P(("tm", "head"), None), P("tm", "head"), P("tm", "head")),
        check_vma=False,
    )
```

time: 175 us -> 55.1 us (0.31)
  the two profiles are of different devices: /device:TPU:1 before, /device:TPU:2 now
where the time goes in v1:
time: 55.1 us; the launch traced here: 54.9 us
  Pallas kernels  48.2 us (87%)
  local copies, waits for them, and re-layouts  5.99 us (11%)
  between operations  0.67 us (1%)
    pallas_call x1, Pallas kernels, on_device(): pl.pallas_call(functools.partial(kernel, plan), out_shape=(jax.ShapeDtype...  48.2 us
    unnamed x16, local copies, waits for them, and re-layouts  5.99 us

profile of v1, /device:TPU:2, one launch (start us, length us, event | category | flops | bytes accessed | tf_op | source)
XLA Modules:
  0.0 54.9 jit_solution(1084572290985997344)
XLA Ops:
  0.6 0.0 copy-start.3
  0.6 0.0 copy-start.4
  0.7 0.0 copy-start.5
  0.7 0.7 %copy-done.3 = f32[1024,1]{0,1:T(1,128)S(1)} copy-done((f32[1024,1]{0,1:T(1,128)S(1)}, f32[1024,1]{0,1:T(1,128)}, u32[]{:S(2)}) %copy-start.3) | copy-done | bytes 4120
  1.3 0.0 copy-done.4
  1.3 0.0 copy-done.5
  1.3 0.0 copy-start
  1.3 1.0 %copy-done = bf16[1024,256]{1,0:T(8,128)(2,1)S(1)} copy-done((bf16[1024,256]{1,0:T(8,128)(2,1)S(1)}, bf16[1024,256]{1,0:T(8,128)(2,1)}, u32[]{:S(2)}) %copy-start) | copy-done | bytes 524312
  2.4 0.0 copy-start.1
  2.4 0.9 %copy-done.1 = bf16[1024,64]{0,1:T(8,128)(2,1)S(1)} copy-done((bf16[1024,64]{0,1:T(8,128)(2,1)S(1)}, bf16[1024,64]{0,1:T(8,128)(2,1)}, u32[]{:S(2)}) %copy-start.1) | copy-done | bytes 131096
  3.3 0.0 copy-start.2
  3.3 0.9 %copy-done.2 = bf16[1024,64]{0,1:T(8,128)(2,1)S(1)} copy-done((bf16[1024,64]{0,1:T(8,128)(2,1)S(1)}, bf16[1024,64]{0,1:T(8,128)(2,1)}, u32[]{:S(2)}) %copy-start.2) | copy-done | bytes 131096
  4.2 48.2 %shard_map.93 = (bf16[64,1024]{1,0:T(8,128)(2,1)S(1)}, f32[16,256]{1,0:T(8,128)S(1)}, f32[8,128]{1,0:T(8,128)S(1)}, f32[64,64]{1,0:T(8,128)S(1)}) custom-call(bf16[64,1024]{1,0:T(8,128)(2,1)S(1)} %bitcast.8, bf16[64,1024]{1,0:T(8,128)(2,1)S(1)} %bitcast.9, bf16[1024,256]{1,0:T(8,128)(2,1)S(1)} %copy-done, f32[8,128]{1,0:T(8,128)S(1)} %bitcast.10, ...), custom_call_target="tpu_custom_call" | custom-call | tf_op jit(solution)/shard_map/pallas_call | solution.py:472
  52.4 0.7 %copy.14 = bf16[1024,64]{0,1:T(8,128)(2,1)} copy(bf16[1024,64]{0,1:T(8,128)(2,1)S(1)} %bitcast.7) | data formatting | bytes 262144
  53.1 0.6 %copy.15 = f32[16,256]{1,0:T(8,128)} copy(f32[16,256]{1,0:T(8,128)S(1)} %get-tuple-element.17) | data formatting | bytes 32768
  53.7 0.6 %copy.16 = f32[1024,1]{0,1:T(1,128)} copy(f32[1024,1]{0,1:T(1,128)S(1)} %bitcast.11) | data formatting | bytes 8192
  54.2 0.6 %copy.17 = f32[64,64]{1,0:T(8,128)} copy(f32[64,64]{1,0:T(8,128)S(1)} %get-tuple-element.19) | data formatting | bytes 32768
Async XLA Ops:
  0.6 0.7 %copy-start.3 = (f32[1024,1]{0,1:T(1,128)S(1)}, f32[1024,1]{0,1:T(1,128)}, u32[]{:S(2)}) copy-start(f32[1024,1]{0,1:T(1,128)} %param.8) | copy-start | bytes 12292
  0.6 0.7 %copy-start.4 = (s32[32,1]{0,1:T(1,128)S(1)}, s32[32,1]{0,1:T(1,128)}, u32[]{:S(2)}) copy-start(s32[32,1]{0,1:T(1,128)} %param.10) | copy-start | bytes 388
  0.7 0.7 %copy-start.5 = (s32[32,1]{0,1:T(1,128)S(1)}, s32[32,1]{0,1:T(1,128)}, u32[]{:S(2)}) copy-start(s32[32,1]{0,1:T(1,128)} %param.11) | copy-start | bytes 388
  1.3 1.0 %copy-start = (bf16[1024,256]{1,0:T(8,128)(2,1)S(1)}, bf16[1024,256]{1,0:T(8,128)(2,1)}, u32[]{:S(2)}) copy-start(bf16[1024,256]{1,0:T(8,128)(2,1)} %bc_hbm.1) | copy-start | bytes 1572868
  2.4 0.9 %copy-start.1 = (bf16[1024,64]{0,1:T(8,128)(2,1)S(1)}, bf16[1024,64]{0,1:T(8,128)(2,1)}, u32[]{:S(2)}) copy-start(bf16[1024,64]{0,1:T(8,128)(2,1)} %param.6) | copy-start | bytes 393220
  3.3 0.9 %copy-start.2 = (bf16[1024,64]{0,1:T(8,128)(2,1)S(1)}, bf16[1024,64]{0,1:T(8,128)(2,1)}, u32[]{:S(2)}) copy-start(bf16[1024,64]{0,1:T(8,128)(2,1)} %param.9) | copy-start | bytes 393220

commit v2 on v1

v2 whole, which is shorter than its diff:
```python
import functools

import jax
import jax.numpy as jnp
from jax import lax
from jax.experimental import pallas as pl
from jax.experimental.pallas import tpu as pltpu
from jax.sharding import PartitionSpec as P

MESH = pl.DeviceIdType.MESH
F32 = jnp.float32
BF16 = jnp.bfloat16
NEWS_DEV = 64
NQ = 32
L = 128


def nn(a, b):
    return lax.dot_general(a, b, (((1,), (0,)), ((), ())), preferred_element_type=F32)


def nt(a, b):
    return lax.dot_general(a, b, (((1,), (1,)), ((), ())), preferred_element_type=F32)


def split2(v):
    hi = v.astype(BF16)
    return hi, (v - hi.astype(F32)).astype(BF16)


def split3(v):
    one = v.astype(BF16).astype(F32)
    two = (v - one).astype(BF16).astype(F32)
    return one, two, v - one - two


def scaled(tiles, tile):
    return (tiles.reshape(8, 8, L) * tile[None]).reshape(64, L)


def iota(shape, dim):
    return lax.broadcasted_iota(jnp.int32, shape, dim)


class Plan:
    def __init__(self, tm, groups, x, y, slots):
        self.tm, self.groups, self.x, self.y, self.slots = tm, groups, x, y, slots
        self.size = tm // groups
        self.block = 1024 // (x * y * 2)
        self.blocks = L // (2 * self.block)
        self.chunks = 8 // x


def kernel(
    plan,
    x_hbm, dy_hbm, bc_hbm, la_hbm, own_hbm, loc_hbm,
    xg_ref, bcg_ref, dla_ref, news_ref,
    xv, dyv, bcv, lav, ownv, locv,
    xyd, col_v, st_loc, scale_v, rows_v,
    loc_bc, dbc, crecv, csum, xrecv, ysum, yrecv,
    y_loc, dx_loc, st2, place_v, ids_v, vx_v, ve,
    g_in, s_in, whole_s, whole_r, edge_v, ns, nr,
    in_sem, g_ss, g_rs, s_ss, s_rs, w_ss, w_rs,
    c_ss, c_rs, x_ss, x_rs, y_ss, y_rs, n_ss, n_rs,
):
    nz, ny, nx = plan.tm, plan.y, plan.x
    zi = lax.axis_index("tm")
    hi_ = lax.axis_index("head")
    core = lax.rem(hi_, 2)
    yi = lax.rem(hi_ // 2, ny)
    xi = hi_ // (2 * ny)

    def head(x, y, c):
        return (x * ny + y) * 2 + c

    def at_z(z):
        return (z, hi_)

    def at_head(h):
        return (zi, h)

    ng, gs = plan.groups, plan.size
    group, place_in = zi // gs, lax.rem(zi, gs)
    collects = (place_in == 0) | (place_in == gs - 1)
    twin = at_head(head(xi, yi, 1 - core))

    loads = [
        pltpu.make_async_copy(src, dst, in_sem.at[k])
        for k, (src, dst) in enumerate(
            ((la_hbm, lav), (dy_hbm, dyv), (bc_hbm, bcv), (x_hbm, xv), (own_hbm, ownv), (loc_hbm, locv))
        )
    ]
    for load in loads:
        load.start()

    barrier = pltpu.get_barrier_semaphore()
    greeted = [at_z(lax.rem(zi + d, nz)) for d in range(1, nz)]
    greeted += [twin]
    greeted += [at_head(head(lax.rem(xi + d, nx), yi, core)) for d in range(1, nx)]
    greeted += [at_head(head(xi, lax.rem(yi + d, ny), core)) for d in range(1, ny)]
    for device in greeted:
        pl.semaphore_signal(barrier, inc=1, device_id=device, device_id_type=MESH)

    up = jnp.where(iota((L, L), 0) <= iota((L, L), 1), 1.0, 0.0).astype(BF16)
    down = jnp.where(iota((L, L), 0) >= iota((L, L), 1), 1.0, 0.0).astype(BF16)
    loads[0].wait()
    parts = split3(lav[...])
    sums = nn(jnp.concatenate([*parts, jnp.zeros((8, L), F32)], axis=0).astype(BF16), up)
    cums = sums[0:8] + sums[8:16] + sums[16:24]
    tot = jnp.broadcast_to(cums[:, L - 1 : L], (8, L))
    after = jnp.exp(cums)
    before = jnp.exp(tot - cums)
    chunk_decay = jnp.exp(tot)
    tots = [tot[c : c + 1] for c in range(8)]
    run = jnp.zeros((1, L), F32)
    for c in range(8):
        scale_v[0, c] = jnp.broadcast_to(jnp.exp(run), (8, L))
        run = run + tots[c]
    device_decay = jnp.exp(run)
    run = jnp.zeros((1, L), F32)
    for c in reversed(range(8)):
        scale_v[1, c] = jnp.broadcast_to(jnp.exp(run), (8, L))
        run = run + tots[c]
    decay_tile = jnp.broadcast_to(device_decay, (8, L))

    def in_group(buf, sems, q):
        return pltpu.make_async_remote_copy(
            src_ref=buf.at[place_in], dst_ref=buf.at[place_in], send_sem=sems[0].at[q], recv_sem=sems[1].at[place_in],
            device_id=at_z(group * gs + q), device_id_type=MESH,
        )

    def arrived(buf, sems, q):
        pltpu.make_async_remote_copy(
            src_ref=buf.at[q], dst_ref=buf.at[q], send_sem=sems[0].at[q], recv_sem=sems[1].at[q],
            device_id=twin, device_id_type=MESH,
        ).wait_recv()

    g_sems, s_sems = (g_ss, g_rs), (s_ss, s_rs)

    def takes_g(q):
        return (q != place_in) & ((q < place_in) | (q == gs - 1))

    def takes_s(q):
        return (q != place_in) & ((q > place_in) | (q == 0))

    loads[1].wait()
    loads[2].wait()
    back = jnp.zeros((64, L), F32)
    for c in reversed(range(8)):
        part = slice(c * L, (c + 1) * L)
        hi, lo = split2(dyv[:, part].astype(F32) * after[c : c + 1])
        cm = bcv[part, L : 2 * L]
        st_loc[1, c] = back
        back = back * chunk_decay[c : c + 1] + nn(
            jnp.concatenate([hi, lo], axis=1), jnp.concatenate([cm, cm], axis=0)
        )
    g_in[place_in, 0:64] = back
    g_in[place_in, 64:72] = decay_tile

    pl.semaphore_wait(barrier, len(greeted))

    for q in reversed(range(gs)):

        @pl.when(takes_g(q))
        def _():
            in_group(g_in, g_sems, q).start()

    loads[3].wait()
    state = jnp.zeros((64, L), F32)
    for c in range(8):
        part = slice(c * L, (c + 1) * L)
        hi, lo = split2(xv[:, part].astype(F32) * before[c : c + 1])
        bm = bcv[part, 0:L]
        st_loc[0, c] = state
        state = state * chunk_decay[c : c + 1] + nn(
            jnp.concatenate([hi, lo], axis=1), jnp.concatenate([bm, bm], axis=0)
        )
    st_loc[0, 8] = state
    s_in[place_in, 0:64] = state
    s_in[place_in, 64:72] = decay_tile
    for q in range(gs):

        @pl.when(takes_s(q))
        def _():
            in_group(s_in, s_sems, q).start()

    big = jnp.concatenate([cums, after, before, jnp.zeros((L - 24, L), F32)], axis=0).T
    lower = iota((L, L), 0) >= iota((L, L), 1)
    upper = iota((L, L), 0) <= iota((L, L), 1)
    rows_v[0] = after
    rows_v[1] = before

    def local(c):
        part = slice(c * L, (c + 1) * L)
        bm, cm = bcv[part, 0:L], bcv[part, L : 2 * L]
        xt, dyt = xv[:, part], dyv[:, part]
        xf, dyf = xt.astype(F32), dyt.astype(F32)
        x2 = jnp.concatenate([xf, xf], axis=0).T.astype(BF16)
        dy2 = jnp.concatenate([dyf, dyf], axis=0).T.astype(BF16)
        xyd[0, c] = dy2
        xyd[1, c] = x2
        col = jnp.broadcast_to(big[:, c : c + 1], (L, L))
        col_v[0, c] = jnp.broadcast_to(big[:, 8 + c : 9 + c], (L, L))
        col_v[1, c] = jnp.broadcast_to(big[:, 16 + c : 17 + c], (L, L))
        row = jnp.broadcast_to(cums[c : c + 1], (L, L))
        m = jnp.exp(jnp.where(lower, col - row, -1e30))
        mt = jnp.exp(jnp.where(upper, row - col, -1e30))
        w = split2(m * nt(cm, bm))
        q = split2(m * nn(dy2[:, 0:64], xt))
        qt = split2(mt * nn(x2[:, 0:64], dyt))
        loc_bc[1, c] = nn(jnp.concatenate(qt, axis=1), jnp.concatenate([cm, cm], axis=0))
        loc_bc[0, c] = nn(jnp.concatenate(q, axis=1), jnp.concatenate([bm, bm], axis=0))
        y_loc[c] = nt(jnp.concatenate([xt, xt], axis=1), jnp.concatenate(w, axis=1))
        dx_loc[c] = nn(jnp.concatenate([dyt, dyt], axis=1), jnp.concatenate(w, axis=0))

    for c in range(8):
        local(c)

    def spans():
        return [(o, 2 * o <= ng) for o in range(1, ng)]

    def whole_copy(o, q):
        to = lax.rem(group + o, ng)
        kind = 1 - (group + o) // ng
        return pltpu.make_async_remote_copy(
            src_ref=whole_s.at[kind], dst_ref=whole_r.at[group], send_sem=w_ss.at[o, q], recv_sem=w_rs.at[group],
            device_id=at_z(to * gs + q), device_id_type=MESH,
        )

    def sender(up):
        return place_in == (gs - 1 if up else 0)

    @pl.when(collects)
    def _():
        for q in range(gs):

            @pl.when(q != place_in)
            def _():
                arrived(g_in, g_sems, q)

        decay = jnp.ones((8, L), F32)
        total = jnp.zeros((64, L), F32)
        for q in reversed(range(gs)):
            total = g_in[q, 0:64] + scaled(total, g_in[q, 64:72])
            decay = decay * g_in[q, 64:72]
        whole_s[0, 0:64] = total
        whole_s[0, 64:72] = decay
        whole_s[1, 64:72] = decay
        for o, up in spans():
            for q in range(gs) if up else reversed(range(gs)):

                @pl.when(sender(up) & (lax.rem(group + o, ng) < group))
                def _():
                    whole_copy(o, q).start()

        for q in range(gs):

            @pl.when(q != place_in)
            def _():
                arrived(s_in, s_sems, q)

        total = jnp.zeros((64, L), F32)
        for q in range(gs):
            total = s_in[q, 0:64] + scaled(total, s_in[q, 64:72])
        whole_s[1, 0:64] = total
        for o, up in spans():
            for q in range(gs) if up else reversed(range(gs)):

                @pl.when(sender(up) & (lax.rem(group + o, ng) > group))
                def _():
                    whole_copy(o, q).start()

    ns_rows = nz * plan.slots
    loads[4].wait()
    loads[5].wait()
    owner_row = ownv[...]
    named = jnp.where(iota((16, NQ), 0) == owner_row, 1.0, 0.0)
    earlier = jnp.where(iota((NQ, NQ), 0) < iota((NQ, NQ), 1), 1.0, 0.0)
    rank = jnp.sum(named * nn(named.astype(BF16), earlier.astype(BF16)), axis=0, keepdims=True)
    slot = owner_row.astype(F32) * plan.slots + rank
    spread = jnp.where(iota((NQ, 1024), 0) == iota((NQ, 1024), 1) // NQ, 1.0, 0.0).astype(BF16)
    slot_t = nn(jnp.broadcast_to(slot, (16, NQ)).astype(BF16), spread)
    for c in range(8):
        hit = slot_t[0:1, c * L : (c + 1) * L] == iota((ns_rows, L), 0).astype(F32)
        place_v[c] = jnp.where(hit, 1.0, 0.0).astype(BF16)
    hit = slot == iota((ns_rows, NQ), 0).astype(F32)
    ids = jnp.sum(jnp.where(hit, locv[...].astype(F32) + 1.0, 0.0), axis=1, keepdims=True)
    ids_v[...] = jnp.where(iota((ns_rows, L), 1) >= 64, ids, 0.0)

    def whole_arrived(a):
        pltpu.make_async_remote_copy(
            src_ref=whole_s.at[0], dst_ref=whole_r.at[a], send_sem=w_ss.at[0, 0], recv_sem=w_rs.at[a],
            device_id=twin, device_id_type=MESH,
        ).wait_recv()

    def state_edge():
        edge_v[0] = jnp.zeros((64, L), F32)
        for a in range(ng):

            @pl.when(a < group)
            def _():
                whole_arrived(a)
                edge_v[0] = whole_r[a, 0:64] + scaled(edge_v[0], whole_r[a, 64:72])

        for q in range(gs):

            @pl.when((q < place_in) & (place_in != gs - 1))
            def _():
                arrived(s_in, s_sems, q)

            @pl.when(q < place_in)
            def _():
                edge_v[0] = s_in[q, 0:64] + scaled(edge_v[0], s_in[q, 64:72])

    def gradient_edge():
        edge_v[1] = jnp.zeros((64, L), F32)
        for a in reversed(range(ng)):

            @pl.when(a > group)
            def _():
                whole_arrived(a)
                edge_v[1] = whole_r[a, 0:64] + scaled(edge_v[1], whole_r[a, 64:72])

        for q in reversed(range(gs)):

            @pl.when((q > place_in) & (place_in != 0))
            def _():
                arrived(g_in, g_sems, q)

            @pl.when(q > place_in)
            def _():
                edge_v[1] = g_in[q, 0:64] + scaled(edge_v[1], g_in[q, 64:72])

    def with_edge(kind, c, edge):
        return st_loc[kind, c] + scaled(edge, scale_v[kind, c])

    span = plan.chunks
    steps = [lax.rem(xi + d, nx) for d in ([2, 1, 3] if nx == 4 else range(1, nx))] + [xi]
    order = [t * span + i for t in steps for i in range(span)]

    def core_copy(kind, c, k):
        return pltpu.make_async_remote_copy(
            src_ref=dbc.at[kind, c, :, 1 - core], dst_ref=crecv.at[kind, c],
            send_sem=c_ss.at[kind, k], recv_sem=c_rs.at[kind, k], device_id=twin, device_id_type=MESH,
        )

    def x_copy(kind, to):
        return pltpu.make_async_remote_copy(
            src_ref=csum.at[kind, pl.ds(to * span, span)], dst_ref=xrecv.at[kind, xi],
            send_sem=x_ss.at[kind, to], recv_sem=x_rs.at[kind, xi],
            device_id=at_head(head(to, yi, core)), device_id_type=MESH,
        )

    def y_copy(kind, d):
        to = lax.rem(yi + d, ny)
        return pltpu.make_async_remote_copy(
            src_ref=ysum.at[kind, to], dst_ref=yrecv.at[kind, yi], send_sem=y_ss.at[kind, d], recv_sem=y_rs.at[kind, yi],
            device_id=at_head(head(xi, to, core)), device_id_type=MESH,
        )

    def over_cores_and_out(kind):
        for n, to in enumerate(steps):
            for i in range(span):
                k = n * span + i
                c = order[k]
                core_copy(kind, c, k).wait_recv()
                csum[kind, c] = dbc[kind, c, :, core] + crecv[kind, c]
            if n < nx - 1:
                x_copy(kind, to).start()

    news_order = sorted(range(1, nz), key=lambda d: -min(d, nz - d))
    y_order = sorted(range(1, ny), key=lambda d: -min(d, ny - d))

    def over_x_and_out(kind):
        total = csum[kind, pl.ds(xi * span, span)]
        for d in range(1, nx):
            source = lax.rem(xi + d, nx)
            pltpu.make_async_remote_copy(
                src_ref=xrecv.at[kind, source], dst_ref=xrecv.at[kind, source],
                send_sem=x_ss.at[kind, 0], recv_sem=x_rs.at[kind, source], device_id=twin, device_id_type=MESH,
            ).wait_recv()
            total = total + xrecv[kind, source]
        ysum[kind] = total.reshape(ny, plan.block, L)
        for d in y_order:
            y_copy(kind, d).start()

    def over_y(kind):
        total = ysum[kind, yi]
        for d in y_order:
            source = lax.rem(yi + d, ny)
            pltpu.make_async_remote_copy(
                src_ref=ysum.at[kind, 0], dst_ref=yrecv.at[kind, source],
                send_sem=y_ss.at[kind, 0], recv_sem=y_rs.at[kind, source], device_id=twin, device_id_type=MESH,
            ).wait_recv()
            total = total + yrecv[kind, source]
        bcg_ref[:, pl.ds(pl.multiple_of((1 - kind) * L, L), L)] = total

    def finish_dx(c, acc):
        part = slice(c * L, (c + 1) * L)
        dxs = nt(st2[1, c], bcv[part, 0:L])
        dxt = dx_loc[c] + rows_v[1, c : c + 1] * (dxs[0:64] + dxs[64:128])
        hi, lo = split2(dxt)
        xg_ref[:, part] = hi
        none = jnp.zeros((64, L), BF16)
        both = jnp.concatenate(
            [jnp.concatenate([hi, none], axis=0), jnp.concatenate([lo, none], axis=0)], axis=1
        )
        place = place_v[c]
        vx_v[c : c + 1] = jnp.sum(xv[:, part].astype(F32) * dxt, axis=0, keepdims=True)
        return acc + nt(jnp.concatenate([place, place], axis=1), both)

    def news_copy(d):
        to = lax.rem(zi + d, nz)
        return pltpu.make_async_remote_copy(
            src_ref=ns.at[to], dst_ref=nr.at[zi], send_sem=n_ss.at[d], recv_sem=n_rs.at[zi],
            device_id=at_z(to), device_id_type=MESH,
        )

    first = (group + 1) // ng
    shape = (plan.blocks, 2, plan.block, L)

    def phase(i, carried):
        kind = first + i - 2 * first * i
        pl.when(kind == 0)(state_edge)
        pl.when(kind == 1)(gradient_edge)
        edge = edge_v[kind]
        for k, c in enumerate(order):
            st = jnp.concatenate(split2(with_edge(kind, c, edge)), axis=0)
            st2[kind, c] = st
            dbc[kind, c] = (loc_bc[kind, c] + col_v[kind, c] * nn(xyd[kind, c], st)).reshape(shape)
            core_copy(kind, c, k).start()
        over_cores_and_out(kind)

        @pl.when(kind == 1)
        def _():
            acc = ids_v[...]
            for c in range(8):
                acc = finish_dx(c, acc)
            ns[...] = acc.reshape(nz, plan.slots, L)
            for d in news_order:
                news_copy(d).start()
            nr[zi] = ns[zi]

        return carried

    lax.fori_loop(0, 2, phase, 0)
    over_x_and_out(first)

    start, carry = edge_v[0], edge_v[1]
    for c in range(8):
        part = slice(c * L, (c + 1) * L)
        ys = nt(st2[0, c], bcv[part, L : 2 * L])
        yt = y_loc[c] + rows_v[0, c : c + 1] * (ys[0:64] + ys[64:128])
        vy = jnp.sum(dyv[:, part].astype(F32) * yt, axis=0, keepdims=True)
        if c < 7:
            end = with_edge(0, c + 1, start)
        else:
            end = st_loc[0, 8] + scaled(start, decay_tile)
        ve[c : c + 1, 0:L] = vy - vx_v[c : c + 1]
        ve[c : c + 1, L : 2 * L] = jnp.sum(with_edge(1, c, carry) * end, axis=0, keepdims=True)
    over_x_and_out(1 - first)
    parts = split3(ve[...])
    sums = nn(
        jnp.concatenate([*parts, jnp.zeros((8, 2 * L), F32)], axis=0).astype(BF16),
        jnp.concatenate([down, jnp.ones((L, L), BF16)], axis=0),
    )
    dla_ref[...] = sums[0:8] + sums[8:16] + sums[16:24]
    over_y(first)

    for d in range(1, nz):
        source = lax.rem(zi + nz - d, nz)
        pltpu.make_async_remote_copy(
            src_ref=ns.at[0], dst_ref=nr.at[source], send_sem=n_ss.at[d], recv_sem=n_rs.at[source],
            device_id=at_z(source), device_id_type=MESH,
        ).wait_recv()
    tiles = nr[...].reshape(ns_rows, L)
    lane = iota((ns_rows, L), 1)
    row_hit = jnp.where((lane >= 64) & (tiles == (lane - 63).astype(F32)), 1.0, 0.0).T.astype(BF16)
    hi, lo = split2(tiles)
    news_ref[...] = (nn(row_hit, hi) + nn(row_hit, lo))[64:128, 0:64]

    over_y(1 - first)

    for q in range(gs):

        @pl.when(takes_g(q))
        def _():
            in_group(g_in, g_sems, q).wait_send()

        @pl.when(takes_s(q))
        def _():
            in_group(s_in, s_sems, q).wait_send()

        for o, up in spans():

            @pl.when(sender(up))
            def _():
                whole_copy(o, q).wait_send()

    for d in range(1, nz):
        news_copy(d).wait_send()
    for kind in range(2):
        for k, c in enumerate(order):
            core_copy(kind, c, k).wait_send()
        for to in steps[:-1]:
            x_copy(kind, to).wait_send()
        for d in range(1, ny):
            y_copy(kind, d).wait_send()


def on_device(plan, xs, bc, log_decay, out_grad, news_owner, news_local):
    rows = plan.tm * plan.slots
    dma = pltpu.SemaphoreType.DMA
    vm = pltpu.VMEM
    shapes = (
        jax.ShapeDtypeStruct((64, 1024), BF16),
        jax.ShapeDtypeStruct((plan.block, 2 * L), F32),
        jax.ShapeDtypeStruct((8, L), F32),
        jax.ShapeDtypeStruct((NEWS_DEV, 64), F32),
    )
    slab = (plan.blocks, plan.block, L)
    ng, gs, nx, ny = plan.groups, plan.size, plan.x, plan.y
    scratch = [
        vm((64, 1024), BF16), vm((64, 1024), BF16), vm((1024, 2 * L), BF16), vm((8, L), F32),
        vm((1, NQ), jnp.int32), vm((1, NQ), jnp.int32),
        vm((2, 8, L, L), BF16), vm((2, 8, L, L), F32), vm((2, 9, 64, L), F32), vm((2, 8, 8, L), F32), vm((2, 8, L), F32),
        vm((2, 8, L, L), F32), vm((2, 8, plan.blocks, 2, plan.block, L), F32),
        vm((2, 8, *slab), F32), vm((2, 8, *slab), F32), vm((2, nx, plan.chunks, *slab), F32),
        vm((2, ny, plan.block, L), F32), vm((2, ny, plan.block, L), F32),
        vm((8, 64, L), F32), vm((8, 64, L), F32), vm((2, 8, L, L), BF16),
        vm((8, rows, L), BF16), vm((rows, L), F32), vm((8, L), F32), vm((8, 2 * L), F32),
        vm((gs, 72, L), F32), vm((gs, 72, L), F32), vm((2, 72, L), F32), vm((ng, 72, L), F32), vm((2, 64, L), F32),
        vm((plan.tm, plan.slots, L), F32), vm((plan.tm, plan.slots, L), F32),
        dma((6,)),
        dma((gs,)), dma((gs,)), dma((gs,)), dma((gs,)), dma((ng, gs)), dma((ng,)),
        dma((2, 8)), dma((2, 8)), dma((2, nx)), dma((2, nx)), dma((2, ny)), dma((2, ny)),
        dma((plan.tm,)), dma((plan.tm,)),
    ]
    anywhere = pl.BlockSpec(memory_space=pl.ANY)
    xg, bcg, dla, news = pl.pallas_call(
        functools.partial(kernel, plan),
        out_shape=shapes,
        in_specs=[anywhere] * 6,
        out_specs=(pl.BlockSpec(memory_space=pltpu.VMEM),) * 4,
        scratch_shapes=scratch,
        compiler_params=pltpu.CompilerParams(
            collective_id=0, has_side_effects=True, vmem_limit_bytes=55000 * 1024
        ),
    )(
        xs.T, out_grad.T, bc, log_decay.reshape(8, L), news_owner.reshape(1, NQ), news_local.reshape(1, NQ)
    )
    return xg.T, bcg, dla.reshape(1024, 1), news


def solution(mesh):
    tm, heads = mesh.shape["tm"], mesh.shape["head"]
    plan = Plan(tm, 3, 4, heads // 8, 8 if tm == 12 else 32)
    return jax.shard_map(
        functools.partial(on_device, plan),
        mesh=mesh,
        in_specs=(
            P("tm", "head"), P("tm", None), P("tm", "head"), P("tm", "head"), P("tm", None), P("tm", None),
        ),
        out_specs=(P("tm", "head"), P(("tm", "head"), None), P("tm", "head"), P("tm", "head")),
        check_vma=False,
    )
```

time: 55.1 us -> 49.2 us (0.89)
  the two profiles are of different devices: /device:TPU:2 before, /device:TPU:1 now
where the time goes in v2:
time: 49.2 us; the launch traced here: 49 us
  Pallas kernels  45.2 us (92%)
  local copies, waits for them, and re-layouts  3.14 us (6%)
  between operations  0.67 us (1%)
    pallas_call x1, Pallas kernels, on_device(): pl.pallas_call(functools.partial(kernel, plan), out_shape=shapes, in_spec...  45.2 us
    unnamed x10, local copies, waits for them, and re-layouts  3.14 us

profile of v2, /device:TPU:1, one launch (start us, length us, event | category | flops | bytes accessed | tf_op | source)
XLA Modules:
  0.0 49.0 jit_solution(1010361811483730946)
XLA Ops:
  0.6 0.0 copy-start
  0.6 0.0 copy-start.1
  0.7 0.0 copy-start.2
  0.7 0.7 %copy-done = f32[1024,1]{0,1:T(1,128)S(1)} copy-done((f32[1024,1]{0,1:T(1,128)S(1)}, f32[1024,1]{0,1:T(1,128)}, u32[]{:S(2)}) %copy-start) | copy-done | bytes 4120
  1.3 0.0 copy-done.1
  1.3 0.0 copy-done.2
  1.3 45.2 %shard_map.93 = (bf16[64,1024]{1,0:T(8,128)(2,1)S(1)}, f32[16,256]{1,0:T(8,128)S(1)}, f32[8,128]{1,0:T(8,128)S(1)}, f32[64,64]{1,0:T(8,128)S(1)}) custom-call(bf16[64,1024]{1,0:T(8,128)(2,1)} %bitcast.12, bf16[64,1024]{1,0:T(8,128)(2,1)} %bitcast.13, bf16[1024,256]{1,0:T(8,128)(2,1)} %bc_hbm.1, f32[8,128]{1,0:T(8,128)S(1)} %bitcast.8, s32[1,32]{1,0:T(1,128)S(1)} %bitcast.10, ...), custom_call_target="tpu_custom_call" | custom-call | tf_op jit(solution)/shard_map/pallas_call | solution.py:540
  46.5 0.7 %copy.14 = bf16[1024,64]{0,1:T(8,128)(2,1)} copy(bf16[1024,64]{0,1:T(8,128)(2,1)S(1)} %bitcast.7) | data formatting | bytes 262144
  47.2 0.6 %copy.15 = f32[16,256]{1,0:T(8,128)} copy(f32[16,256]{1,0:T(8,128)S(1)} %get-tuple-element.17) | data formatting | bytes 32768
  47.8 0.6 %copy.16 = f32[1024,1]{0,1:T(1,128)} copy(f32[1024,1]{0,1:T(1,128)S(1)} %bitcast.9) | data formatting | bytes 8192
  48.4 0.6 %copy.17 = f32[64,64]{1,0:T(8,128)} copy(f32[64,64]{1,0:T(8,128)S(1)} %get-tuple-element.19) | data formatting | bytes 32768
Async XLA Ops:
  0.6 0.7 %copy-start = (f32[1024,1]{0,1:T(1,128)S(1)}, f32[1024,1]{0,1:T(1,128)}, u32[]{:S(2)}) copy-start(f32[1024,1]{0,1:T(1,128)} %param.8) | copy-start | bytes 12292
  0.6 0.7 %copy-start.1 = (s32[32,1]{0,1:T(1,128)S(1)}, s32[32,1]{0,1:T(1,128)}, u32[]{:S(2)}) copy-start(s32[32,1]{0,1:T(1,128)} %param.10) | copy-start | bytes 388
  0.7 0.7 %copy-start.2 = (s32[32,1]{0,1:T(1,128)S(1)}, s32[32,1]{0,1:T(1,128)}, u32[]{:S(2)}) copy-start(s32[32,1]{0,1:T(1,128)} %param.11) | copy-start | bytes 388

commit v3 on v2

--- a/solution.py
+++ b/solution.py
@@ -60,7 +60,7 @@
     loc_bc, dbc, crecv, csum, xrecv, ysum, yrecv,
     y_loc, dx_loc, st2, place_v, ids_v, vx_v, ve,
     g_in, s_in, whole_s, whole_r, edge_v, ns, nr,
-    in_sem, g_ss, g_rs, s_ss, s_rs, w_ss, w_rs,
+    ready_g, ready_w, ready_p, in_sem, g_ss, g_rs, s_ss, s_rs, w_ss, w_rs,
     c_ss, c_rs, x_ss, x_rs, y_ss, y_rs, n_ss, n_rs,
 ):
     nz, ny, nx = plan.tm, plan.y, plan.x
@@ -81,7 +81,6 @@
 
     ng, gs = plan.groups, plan.size
     group, place_in = zi // gs, lax.rem(zi, gs)
-    collects = (place_in == 0) | (place_in == gs - 1)
     twin = at_head(head(xi, yi, 1 - core))
 
     loads = [
@@ -94,12 +93,50 @@
         load.start()
 
     barrier = pltpu.get_barrier_semaphore()
-    greeted = [at_z(lax.rem(zi + d, nz)) for d in range(1, nz)]
-    greeted += [twin]
-    greeted += [at_head(head(lax.rem(xi + d, nx), yi, core)) for d in range(1, nx)]
-    greeted += [at_head(head(xi, lax.rem(yi + d, ny), core)) for d in range(1, ny)]
-    for device in greeted:
-        pl.semaphore_signal(barrier, inc=1, device_id=device, device_id_type=MESH)
+    low, high = zi == 0, group == ng - 1
+    bottom, top = place_in == 0, place_in == gs - 1
+
+    def rank(y):
+        return y + y // (ny // 2) * (ny + ny // 2 - 1 - 2 * y)
+
+    def signal(sem, device, when):
+        @pl.when(when)
+        def _():
+            pl.semaphore_signal(sem, inc=1, device_id=device, device_id_type=MESH)
+
+    pairs = [(twin, core == 1)]
+    for d in range(1, nx):
+        to = lax.rem(xi + d, nx)
+        pairs.append((at_head(head(to, yi, core)), to > xi))
+    for d in range(1, ny):
+        to = lax.rem(yi + d, ny)
+        pairs.append((at_head(head(xi, to, core)), rank(to) > rank(yi)))
+
+    for q in range(gs):
+        signal(barrier, at_z(group * gs + q), q > place_in)
+    above = lax.rem(group + 1, ng) * gs
+    below = lax.rem(group + ng - 1, ng) * gs
+    signal(barrier, at_z(above), group + 1 < ng - 1)
+    for q in range(gs):
+        signal(barrier, at_z(above + q), top & (group + 1 < ng - 1))
+        signal(barrier, at_z(nz - gs + q), group < ng - 1)
+    for device, later in pairs:
+        signal(barrier, device, later)
+
+    def await_count(sem, count):
+        @pl.when(count > 0)
+        def _():
+            pl.semaphore_wait(sem, count)
+
+    def flag(value):
+        return jnp.where(value, 1, 0)
+
+    earlier_plane = (1 - core) + xi + rank(yi)
+    later_plane = nx + ny - 1 - earlier_plane
+    greetings = (
+        place_in + earlier_plane + flag(high) * (nz - gs)
+        + flag((group > 0) & (group < ng - 1)) * (1 + gs * flag(bottom))
+    )
 
     up = jnp.where(iota((L, L), 0) <= iota((L, L), 1), 1.0, 0.0).astype(BF16)
     down = jnp.where(iota((L, L), 0) >= iota((L, L), 1), 1.0, 0.0).astype(BF16)
@@ -138,10 +175,10 @@
     g_sems, s_sems = (g_ss, g_rs), (s_ss, s_rs)
 
     def takes_g(q):
-        return (q != place_in) & ((q < place_in) | (q == gs - 1))
+        return (q < place_in) | ((q == gs - 1) & high & (q != place_in))
 
     def takes_s(q):
-        return (q != place_in) & ((q > place_in) | (q == 0))
+        return (q > place_in) | ((q == 0) & (group == 0) & (q != place_in))
 
     loads[1].wait()
     loads[2].wait()
@@ -157,11 +194,17 @@
     g_in[place_in, 0:64] = back
     g_in[place_in, 64:72] = decay_tile
 
-    pl.semaphore_wait(barrier, len(greeted))
-
-    for q in reversed(range(gs)):
-
-        @pl.when(takes_g(q))
+    await_count(barrier, greetings)
+    for q in range(gs):
+        signal(ready_g, at_z(group * gs + q), q < place_in)
+    signal(ready_w, at_z(below + gs - 1), group > 0)
+    signal(ready_w, at_z(0), high)
+    for device, later in pairs:
+        signal(ready_p, device, jnp.logical_not(later))
+
+    for q in range(gs):
+
+        @pl.when(takes_g(q) & (q < place_in))
         def _():
             in_group(g_in, g_sems, q).start()
 
@@ -178,11 +221,61 @@
     st_loc[0, 8] = state
     s_in[place_in, 0:64] = state
     s_in[place_in, 64:72] = decay_tile
-    for q in range(gs):
+
+    @pl.when(takes_s(0))
+    def _():
+        in_group(s_in, s_sems, 0).start()
+
+    await_count(ready_g, gs - 1 - place_in)
+
+    @pl.when(takes_g(gs - 1))
+    def _():
+        in_group(g_in, g_sems, gs - 1).start()
+
+    for q in range(1, gs):
 
         @pl.when(takes_s(q))
         def _():
             in_group(s_in, s_sems, q).start()
+
+    def spans():
+        return [(o, 2 * o <= ng) for o in range(1, ng)]
+
+    def whole_copy(o, q):
+        to = lax.rem(group + o, ng)
+        kind = 1 - (group + o) // ng
+        return pltpu.make_async_remote_copy(
+            src_ref=whole_s.at[kind], dst_ref=whole_r.at[group], send_sem=w_ss.at[o, q], recv_sem=w_rs.at[group],
+            device_id=at_z(to * gs + q), device_id_type=MESH,
+        )
+
+    def sender(up):
+        return place_in == (gs - 1 if up else 0)
+
+    collects_g = (bottom & (group > 0)) | (zi == nz - 1)
+    collects_s = low | (top & (group < ng - 1))
+
+    @pl.when(collects_g)
+    def _():
+        for q in range(gs):
+
+            @pl.when(q != place_in)
+            def _():
+                arrived(g_in, g_sems, q)
+
+        decay = jnp.ones((8, L), F32)
+        total = jnp.zeros((64, L), F32)
+        for q in reversed(range(gs)):
+            total = g_in[q, 0:64] + scaled(total, g_in[q, 64:72])
+            decay = decay * g_in[q, 64:72]
+        whole_s[0, 0:64] = total
+        whole_s[0, 64:72] = decay
+        for o, up in spans():
+            for q in range(gs):
+
+                @pl.when(sender(up) & (lax.rem(group + o, ng) < group))
+                def _():
+                    whole_copy(o, q).start()
 
     big = jnp.concatenate([cums, after, before, jnp.zeros((L - 24, L), F32)], axis=0).T
     lower = iota((L, L), 0) >= iota((L, L), 1)
@@ -216,55 +309,24 @@
     for c in range(8):
         local(c)
 
-    def spans():
-        return [(o, 2 * o <= ng) for o in range(1, ng)]
-
-    def whole_copy(o, q):
-        to = lax.rem(group + o, ng)
-        kind = 1 - (group + o) // ng
-        return pltpu.make_async_remote_copy(
-            src_ref=whole_s.at[kind], dst_ref=whole_r.at[group], send_sem=w_ss.at[o, q], recv_sem=w_rs.at[group],
-            device_id=at_z(to * gs + q), device_id_type=MESH,
-        )
-
-    def sender(up):
-        return place_in == (gs - 1 if up else 0)
-
-    @pl.when(collects)
+    @pl.when(collects_s)
     def _():
         for q in range(gs):
 
             @pl.when(q != place_in)
             def _():
-                arrived(g_in, g_sems, q)
+                arrived(s_in, s_sems, q)
 
         decay = jnp.ones((8, L), F32)
-        total = jnp.zeros((64, L), F32)
-        for q in reversed(range(gs)):
-            total = g_in[q, 0:64] + scaled(total, g_in[q, 64:72])
-            decay = decay * g_in[q, 64:72]
-        whole_s[0, 0:64] = total
-        whole_s[0, 64:72] = decay
-        whole_s[1, 64:72] = decay
-        for o, up in spans():
-            for q in range(gs) if up else reversed(range(gs)):
-
-                @pl.when(sender(up) & (lax.rem(group + o, ng) < group))
-                def _():
-                    whole_copy(o, q).start()
-
-        for q in range(gs):
-
-            @pl.when(q != place_in)
-            def _():
-                arrived(s_in, s_sems, q)
-
         total = jnp.zeros((64, L), F32)
         for q in range(gs):
             total = s_in[q, 0:64] + scaled(total, s_in[q, 64:72])
+            decay = decay * s_in[q, 64:72]
         whole_s[1, 0:64] = total
+        whole_s[1, 64:72] = decay
+        await_count(ready_w, gs * flag(top) + gs * flag(low))
         for o, up in spans():
-            for q in range(gs) if up else reversed(range(gs)):
+            for q in range(gs):
 
                 @pl.when(sender(up) & (lax.rem(group + o, ng) > group))
                 def _():
@@ -304,7 +366,7 @@
 
         for q in range(gs):
 
-            @pl.when((q < place_in) & (place_in != gs - 1))
+            @pl.when((q < place_in) & jnp.logical_not(collects_s))
             def _():
                 arrived(s_in, s_sems, q)
 
@@ -323,7 +385,7 @@
 
         for q in reversed(range(gs)):
 
-            @pl.when((q > place_in) & (place_in != 0))
+            @pl.when((q > place_in) & jnp.logical_not(collects_g))
             def _():
                 arrived(g_in, g_sems, q)
 
@@ -416,6 +478,7 @@
             device_id=at_z(to), device_id_type=MESH,
         )
 
+    await_count(ready_p, later_plane)
     first = (group + 1) // ng
     shape = (plan.blocks, 2, plan.block, L)
 
@@ -429,8 +492,6 @@
             st2[kind, c] = st
             dbc[kind, c] = (loc_bc[kind, c] + col_v[kind, c] * nn(xyd[kind, c], st)).reshape(shape)
             core_copy(kind, c, k).start()
-        over_cores_and_out(kind)
-
         @pl.when(kind == 1)
         def _():
             acc = ids_v[...]
@@ -441,10 +502,11 @@
                 news_copy(d).start()
             nr[zi] = ns[zi]
 
+        over_cores_and_out(kind)
+        over_x_and_out(kind)
         return carried
 
     lax.fori_loop(0, 2, phase, 0)
-    over_x_and_out(first)
 
     start, carry = edge_v[0], edge_v[1]
     for c in range(8):
@@ -458,7 +520,6 @@
             end = st_loc[0, 8] + scaled(start, decay_tile)
         ve[c : c + 1, 0:L] = vy - vx_v[c : c + 1]
         ve[c : c + 1, L : 2 * L] = jnp.sum(with_edge(1, c, carry) * end, axis=0, keepdims=True)
-    over_x_and_out(1 - first)
     parts = split3(ve[...])
     sums = nn(
         jnp.concatenate([*parts, jnp.zeros((8, 2 * L), F32)], axis=0).astype(BF16),
@@ -531,7 +592,7 @@
         vm((8, rows, L), BF16), vm((rows, L), F32), vm((8, L), F32), vm((8, 2 * L), F32),
         vm((gs, 72, L), F32), vm((gs, 72, L), F32), vm((2, 72, L), F32), vm((ng, 72, L), F32), vm((2, 64, L), F32),
         vm((plan.tm, plan.slots, L), F32), vm((plan.tm, plan.slots, L), F32),
-        dma((6,)),
+        *[pltpu.SemaphoreType.REGULAR] * 3, dma((6,)),
         dma((gs,)), dma((gs,)), dma((gs,)), dma((gs,)), dma((ng, gs)), dma((ng,)),
         dma((2, 8)), dma((2, 8)), dma((2, nx)), dma((2, nx)), dma((2, ny)), dma((2, ny)),
         dma((plan.tm,)), dma((plan.tm,)),

time: 49.2 us -> 44.6 us (0.907)
  Pallas kernels: 45.2 us -> 40.2 us
    pallas_call x1, Pallas kernels: 45.2 us -> 40.2 us  [on_device(): pl.pallas_call(functools.partial(kernel, plan), out_shape=shapes, in_spec...]
where the time goes in v3:
time: 44.6 us; the launch traced here: 44 us
  Pallas kernels  40.2 us (90%)
  local copies, waits for them, and re-layouts  3.14 us (7%)
  between operations  0.67 us (2%)
    pallas_call x1, Pallas kernels, on_device(): pl.pallas_call(functools.partial(kernel, plan), out_shape=shapes, in_spec...  40.2 us
    unnamed x10, local copies, waits for them, and re-layouts  3.14 us

profile of v3, /device:TPU:1, one launch (start us, length us, event | category | flops | bytes accessed | tf_op | source)
XLA Modules:
  0.0 44.0 jit_solution(12346284039306638583)
XLA Ops:
  0.6 0.0 copy-start
  0.6 0.0 copy-start.1
  0.7 0.0 copy-start.2
  0.7 0.7 %copy-done = f32[1024,1]{0,1:T(1,128)S(1)} copy-done((f32[1024,1]{0,1:T(1,128)S(1)}, f32[1024,1]{0,1:T(1,128)}, u32[]{:S(2)}) %copy-start) | copy-done | bytes 4120
  1.3 0.0 copy-done.1
  1.3 0.0 copy-done.2
  1.3 40.2 %shard_map.93 = (bf16[64,1024]{1,0:T(8,128)(2,1)S(1)}, f32[16,256]{1,0:T(8,128)S(1)}, f32[8,128]{1,0:T(8,128)S(1)}, f32[64,64]{1,0:T(8,128)S(1)}) custom-call(bf16[64,1024]{1,0:T(8,128)(2,1)} %bitcast.12, bf16[64,1024]{1,0:T(8,128)(2,1)} %bitcast.13, bf16[1024,256]{1,0:T(8,128)(2,1)} %bc_hbm.1, f32[8,128]{1,0:T(8,128)S(1)} %bitcast.8, s32[1,32]{1,0:T(1,128)S(1)} %bitcast.10, ...), custom_call_target="tpu_custom_call" | custom-call | tf_op jit(solution)/shard_map/pallas_call | solution.py:601
  41.5 0.7 %copy.14 = bf16[1024,64]{0,1:T(8,128)(2,1)} copy(bf16[1024,64]{0,1:T(8,128)(2,1)S(1)} %bitcast.7) | data formatting | bytes 262144
  42.1 0.6 %copy.15 = f32[16,256]{1,0:T(8,128)} copy(f32[16,256]{1,0:T(8,128)S(1)} %get-tuple-element.17) | data formatting | bytes 32768
  42.8 0.6 %copy.16 = f32[1024,1]{0,1:T(1,128)} copy(f32[1024,1]{0,1:T(1,128)S(1)} %bitcast.9) | data formatting | bytes 8192
  43.3 0.6 %copy.17 = f32[64,64]{1,0:T(8,128)} copy(f32[64,64]{1,0:T(8,128)S(1)} %get-tuple-element.19) | data formatting | bytes 32768
Async XLA Ops:
  0.6 0.7 %copy-start = (f32[1024,1]{0,1:T(1,128)S(1)}, f32[1024,1]{0,1:T(1,128)}, u32[]{:S(2)}) copy-start(f32[1024,1]{0,1:T(1,128)} %param.8) | copy-start | bytes 12292
  0.6 0.7 %copy-start.1 = (s32[32,1]{0,1:T(1,128)S(1)}, s32[32,1]{0,1:T(1,128)}, u32[]{:S(2)}) copy-start(s32[32,1]{0,1:T(1,128)} %param.10) | copy-start | bytes 388
  0.7 0.7 %copy-start.2 = (s32[32,1]{0,1:T(1,128)S(1)}, s32[32,1]{0,1:T(1,128)}, u32[]{:S(2)}) copy-start(s32[32,1]{0,1:T(1,128)} %param.11) | copy-start | bytes 388

commit v4 on v3

--- a/solution.py
+++ b/solution.py
@@ -53,9 +53,9 @@
 
 def kernel(
     plan,
-    x_hbm, dy_hbm, bc_hbm, la_hbm, own_hbm, loc_hbm,
+    x_hbm, dy_hbm, bc_hbm, lav, ownv, locv,
     xg_ref, bcg_ref, dla_ref, news_ref,
-    xv, dyv, bcv, lav, ownv, locv,
+    xv, dyv, bcv,
     xyd, col_v, st_loc, scale_v, rows_v,
     loc_bc, dbc, crecv, csum, xrecv, ysum, yrecv,
     y_loc, dx_loc, st2, place_v, ids_v, vx_v, ve,
@@ -86,7 +86,7 @@
     loads = [
         pltpu.make_async_copy(src, dst, in_sem.at[k])
         for k, (src, dst) in enumerate(
-            ((la_hbm, lav), (dy_hbm, dyv), (bc_hbm, bcv), (x_hbm, xv), (own_hbm, ownv), (loc_hbm, locv))
+            ((dy_hbm, dyv), (bc_hbm, bcv), (x_hbm, xv))
         )
     ]
     for load in loads:
@@ -94,6 +94,7 @@
 
     barrier = pltpu.get_barrier_semaphore()
     low, high = zi == 0, group == ng - 1
+    wraps = group >= ng - ng // 2
     bottom, top = place_in == 0, place_in == gs - 1
 
     def rank(y):
@@ -120,6 +121,10 @@
     for q in range(gs):
         signal(barrier, at_z(above + q), top & (group + 1 < ng - 1))
         signal(barrier, at_z(nz - gs + q), group < ng - 1)
+    if ng == 4:
+        signal(barrier, at_z(3 * gs - 1), group == 0)
+        for q in range(gs):
+            signal(barrier, at_z(2 * gs + q), top & (group == 0))
     for device, later in pairs:
         signal(barrier, device, later)
 
@@ -137,10 +142,11 @@
         place_in + earlier_plane + flag(high) * (nz - gs)
         + flag((group > 0) & (group < ng - 1)) * (1 + gs * flag(bottom))
     )
+    if ng == 4:
+        greetings = greetings + flag(group == 2) * (1 + gs * flag(top))
 
     up = jnp.where(iota((L, L), 0) <= iota((L, L), 1), 1.0, 0.0).astype(BF16)
     down = jnp.where(iota((L, L), 0) >= iota((L, L), 1), 1.0, 0.0).astype(BF16)
-    loads[0].wait()
     parts = split3(lav[...])
     sums = nn(jnp.concatenate([*parts, jnp.zeros((8, L), F32)], axis=0).astype(BF16), up)
     cums = sums[0:8] + sums[8:16] + sums[16:24]
@@ -175,13 +181,13 @@
     g_sems, s_sems = (g_ss, g_rs), (s_ss, s_rs)
 
     def takes_g(q):
-        return (q < place_in) | ((q == gs - 1) & high & (q != place_in))
+        return (q < place_in) | ((q == gs - 1) & wraps & (q != place_in))
 
     def takes_s(q):
         return (q > place_in) | ((q == 0) & (group == 0) & (q != place_in))
 
+    loads[0].wait()
     loads[1].wait()
-    loads[2].wait()
     back = jnp.zeros((64, L), F32)
     for c in reversed(range(8)):
         part = slice(c * L, (c + 1) * L)
@@ -199,6 +205,8 @@
         signal(ready_g, at_z(group * gs + q), q < place_in)
     signal(ready_w, at_z(below + gs - 1), group > 0)
     signal(ready_w, at_z(0), high)
+    if ng == 4:
+        signal(ready_w, at_z(lax.rem(group + 2, ng) * gs + gs - 1), group > 1)
     for device, later in pairs:
         signal(ready_p, device, jnp.logical_not(later))
 
@@ -208,7 +216,7 @@
         def _():
             in_group(g_in, g_sems, q).start()
 
-    loads[3].wait()
+    loads[2].wait()
     state = jnp.zeros((64, L), F32)
     for c in range(8):
         part = slice(c * L, (c + 1) * L)
@@ -252,7 +260,7 @@
     def sender(up):
         return place_in == (gs - 1 if up else 0)
 
-    collects_g = (bottom & (group > 0)) | (zi == nz - 1)
+    collects_g = (bottom & (group > 0)) | (top & wraps)
     collects_s = low | (top & (group < ng - 1))
 
     @pl.when(collects_g)
@@ -324,7 +332,10 @@
             decay = decay * s_in[q, 64:72]
         whole_s[1, 0:64] = total
         whole_s[1, 64:72] = decay
-        await_count(ready_w, gs * flag(top) + gs * flag(low))
+        told = gs * flag(top) + gs * flag(low)
+        if ng == 4:
+            told = told + gs * flag(top & (group < 2))
+        await_count(ready_w, told)
         for o, up in spans():
             for q in range(gs):
 
@@ -333,8 +344,6 @@
                     whole_copy(o, q).start()
 
     ns_rows = nz * plan.slots
-    loads[4].wait()
-    loads[5].wait()
     owner_row = ownv[...]
     named = jnp.where(iota((16, NQ), 0) == owner_row, 1.0, 0.0)
     earlier = jnp.where(iota((NQ, NQ), 0) < iota((NQ, NQ), 1), 1.0, 0.0)
@@ -569,6 +578,15 @@
             y_copy(kind, d).wait_send()
 
 
+def write_out(a, b, c, d, a_out, b_out, c_out, d_out, sems):
+    pairs = ((a, a_out), (b, b_out), (c, c_out), (d, d_out))
+    copies = [pltpu.make_async_copy(src, dst, sems.at[k]) for k, (src, dst) in enumerate(pairs)]
+    for copy in copies:
+        copy.start()
+    for copy in copies:
+        copy.wait()
+
+
 def on_device(plan, xs, bc, log_decay, out_grad, news_owner, news_local):
     rows = plan.tm * plan.slots
     dma = pltpu.SemaphoreType.DMA
@@ -582,8 +600,7 @@
     slab = (plan.blocks, plan.block, L)
     ng, gs, nx, ny = plan.groups, plan.size, plan.x, plan.y
     scratch = [
-        vm((64, 1024), BF16), vm((64, 1024), BF16), vm((1024, 2 * L), BF16), vm((8, L), F32),
-        vm((1, NQ), jnp.int32), vm((1, NQ), jnp.int32),
+        vm((64, 1024), BF16), vm((64, 1024), BF16), vm((1024, 2 * L), BF16),
         vm((2, 8, L, L), BF16), vm((2, 8, L, L), F32), vm((2, 9, 64, L), F32), vm((2, 8, 8, L), F32), vm((2, 8, L), F32),
         vm((2, 8, L, L), F32), vm((2, 8, plan.blocks, 2, plan.block, L), F32),
         vm((2, 8, *slab), F32), vm((2, 8, *slab), F32), vm((2, nx, plan.chunks, *slab), F32),
@@ -592,17 +609,18 @@
         vm((8, rows, L), BF16), vm((rows, L), F32), vm((8, L), F32), vm((8, 2 * L), F32),
         vm((gs, 72, L), F32), vm((gs, 72, L), F32), vm((2, 72, L), F32), vm((ng, 72, L), F32), vm((2, 64, L), F32),
         vm((plan.tm, plan.slots, L), F32), vm((plan.tm, plan.slots, L), F32),
-        *[pltpu.SemaphoreType.REGULAR] * 3, dma((6,)),
+        *[pltpu.SemaphoreType.REGULAR] * 3, dma((3,)),
         dma((gs,)), dma((gs,)), dma((gs,)), dma((gs,)), dma((ng, gs)), dma((ng,)),
         dma((2, 8)), dma((2, 8)), dma((2, nx)), dma((2, nx)), dma((2, ny)), dma((2, ny)),
         dma((plan.tm,)), dma((plan.tm,)),
     ]
     anywhere = pl.BlockSpec(memory_space=pl.ANY)
-    xg, bcg, dla, news = pl.pallas_call(
+    vmem = pl.BlockSpec(memory_space=pltpu.VMEM)
+    results = pl.pallas_call(
         functools.partial(kernel, plan),
         out_shape=shapes,
-        in_specs=[anywhere] * 6,
-        out_specs=(pl.BlockSpec(memory_space=pltpu.VMEM),) * 4,
+        in_specs=[anywhere] * 3 + [vmem] * 3,
+        out_specs=(vmem,) * 4,
         scratch_shapes=scratch,
         compiler_params=pltpu.CompilerParams(
             collective_id=0, has_side_effects=True, vmem_limit_bytes=55000 * 1024
@@ -610,6 +628,14 @@
     )(
         xs.T, out_grad.T, bc, log_decay.reshape(8, L), news_owner.reshape(1, NQ), news_local.reshape(1, NQ)
     )
+    xg, bcg, dla, news = pl.pallas_call(
+        write_out,
+        out_shape=shapes,
+        in_specs=[anywhere] * 4,
+        out_specs=(anywhere,) * 4,
+        scratch_shapes=[dma((4,))],
+        compiler_params=pltpu.CompilerParams(vmem_limit_bytes=2**20),
+    )(*results)
     return xg.T, bcg, dla.reshape(1024, 1), news
 
 

time: 44.6 us -> 42.8 us (0.960)
  local copies, waits for them, and re-layouts: 3.14 us -> 0.67 us
  Pallas kernels: 40.2 us -> 40.8 us
    unnamed x10 -> x6, local copies, waits for them, and re-layouts: 3.14 us -> 0.67 us
    pallas_call x0 -> x1, Pallas kernels: none -> 0.71 us  [on_device(): pl.pallas_call(write_out, out_shape=shapes, in_specs=[anywhere] * 4, out_...]
where the time goes in v4:
time: 42.8 us; the launch traced here: 42.2 us
  Pallas kernels  40.8 us (95%)
  local copies, waits for them, and re-layouts  0.67 us (2%)
  between operations  0.67 us (2%)
    pallas_call x1, Pallas kernels, on_device(): pl.pallas_call(functools.partial(kernel, plan), out_shape=shapes, in_spec...  40.1 us

profile of v4, /device:TPU:1, one launch (start us, length us, event | category | flops | bytes accessed | tf_op | source)
XLA Modules:
  0.0 42.2 jit_solution(8045970969320082718)
XLA Ops:
  0.6 0.0 copy-start
  0.6 0.0 copy-start.1
  0.7 0.0 copy-start.2
  0.7 0.7 %copy-done = f32[1024,1]{0,1:T(1,128)S(1)} copy-done((f32[1024,1]{0,1:T(1,128)S(1)}, f32[1024,1]{0,1:T(1,128)}, u32[]{:S(2)}) %copy-start) | copy-done | bytes 4120
  1.3 0.0 copy-done.1
  1.3 0.0 copy-done.2
  1.3 40.1 %shard_map.93 = (bf16[64,1024]{1,0:T(8,128)(2,1)S(1)}, f32[16,256]{1,0:T(8,128)S(1)}, f32[8,128]{1,0:T(8,128)S(1)}, f32[64,64]{1,0:T(8,128)S(1)}) custom-call(bf16[64,1024]{1,0:T(8,128)(2,1)} %bitcast.10, bf16[64,1024]{1,0:T(8,128)(2,1)} %bitcast.11, bf16[1024,256]{1,0:T(8,128)(2,1)} %bc_hbm.1, f32[8,128]{1,0:T(8,128)S(1)} %bitcast.7, s32[1,32]{1,0:T(1,128)S(1)} %bitcast.8, ...), custom_call_target="tpu_custom_call" | custom-call | tf_op jit(solution)/shard_map/pallas_call | solution.py:619
  41.4 0.7 %shard_map.94 = (bf16[64,1024]{1,0:T(8,128)(2,1)}, f32[16,256]{1,0:T(8,128)}, f32[8,128]{1,0:T(8,128)}, f32[64,64]{1,0:T(8,128)}) custom-call(bf16[64,1024]{1,0:T(8,128)(2,1)S(1)} %get-tuple-element.12.a, f32[16,256]{1,0:T(8,128)S(1)} %get-tuple-element.13.b, f32[8,128]{1,0:T(8,128)S(1)} %get-tuple-element.14.c, f32[64,64]{1,0:T(8,128)S(1)} %get-tuple-element.15.d), custom_call_target="tpu_custom_call" | custom-call | tf_op jit(solution)/shard_map/pallas_call | solution.py:631
Async XLA Ops:
  0.6 0.7 %copy-start = (f32[1024,1]{0,1:T(1,128)S(1)}, f32[1024,1]{0,1:T(1,128)}, u32[]{:S(2)}) copy-start(f32[1024,1]{0,1:T(1,128)} %param.8) | copy-start | bytes 12292
  0.6 0.7 %copy-start.1 = (s32[32,1]{0,1:T(1,128)S(1)}, s32[32,1]{0,1:T(1,128)}, u32[]{:S(2)}) copy-start(s32[32,1]{0,1:T(1,128)} %param.10) | copy-start | bytes 388
  0.7 0.7 %copy-start.2 = (s32[32,1]{0,1:T(1,128)S(1)}, s32[32,1]{0,1:T(1,128)}, u32[]{:S(2)}) copy-start(s32[32,1]{0,1:T(1,128)} %param.11) | copy-start | bytes 388

commit v5 on v4

--- a/solution.py
+++ b/solution.py
@@ -407,7 +407,7 @@
 
     span = plan.chunks
     steps = [lax.rem(xi + d, nx) for d in ([2, 1, 3] if nx == 4 else range(1, nx))] + [xi]
-    order = [t * span + i for t in steps for i in range(span)]
+    order = [t * span + i for i in range(span) for t in steps]
 
     def core_copy(kind, c, k):
         return pltpu.make_async_remote_copy(
@@ -415,10 +415,10 @@
             send_sem=c_ss.at[kind, k], recv_sem=c_rs.at[kind, k], device_id=twin, device_id_type=MESH,
         )
 
-    def x_copy(kind, to):
+    def x_copy(kind, to, i):
         return pltpu.make_async_remote_copy(
-            src_ref=csum.at[kind, pl.ds(to * span, span)], dst_ref=xrecv.at[kind, xi],
-            send_sem=x_ss.at[kind, to], recv_sem=x_rs.at[kind, xi],
+            src_ref=csum.at[kind, to * span + i], dst_ref=xrecv.at[kind, xi, i],
+            send_sem=x_ss.at[kind, to * span + i], recv_sem=x_rs.at[kind, xi * span + i],
             device_id=at_head(head(to, yi, core)), device_id_type=MESH,
         )
 
@@ -430,30 +430,31 @@
         )
 
     def over_cores_and_out(kind):
-        for n, to in enumerate(steps):
-            for i in range(span):
-                k = n * span + i
-                c = order[k]
-                core_copy(kind, c, k).wait_recv()
-                csum[kind, c] = dbc[kind, c, :, core] + crecv[kind, c]
-            if n < nx - 1:
-                x_copy(kind, to).start()
+        for k, c in enumerate(order):
+            core_copy(kind, c, k).wait_recv()
+            csum[kind, c] = dbc[kind, c, :, core] + crecv[kind, c]
+            if k % nx < nx - 1:
+                x_copy(kind, steps[k % nx], k // nx).start()
 
     news_order = sorted(range(1, nz), key=lambda d: -min(d, nz - d))
     y_order = sorted(range(1, ny), key=lambda d: -min(d, ny - d))
 
     def over_x_and_out(kind):
-        total = csum[kind, pl.ds(xi * span, span)]
-        for d in range(1, nx):
-            source = lax.rem(xi + d, nx)
-            pltpu.make_async_remote_copy(
-                src_ref=xrecv.at[kind, source], dst_ref=xrecv.at[kind, source],
-                send_sem=x_ss.at[kind, 0], recv_sem=x_rs.at[kind, source], device_id=twin, device_id_type=MESH,
-            ).wait_recv()
-            total = total + xrecv[kind, source]
-        ysum[kind] = total.reshape(ny, plan.block, L)
-        for d in y_order:
-            y_copy(kind, d).start()
+        for i in range(span):
+            total = csum[kind, xi * span + i]
+            for d in range(1, nx):
+                source = lax.rem(xi + d, nx)
+                pltpu.make_async_remote_copy(
+                    src_ref=xrecv.at[kind, source, i], dst_ref=xrecv.at[kind, source, i], send_sem=x_ss.at[kind, 0],
+                    recv_sem=x_rs.at[kind, source * span + i], device_id=twin, device_id_type=MESH,
+                ).wait_recv()
+                total = total + xrecv[kind, source, i]
+            ysum[kind, i * plan.blocks : (i + 1) * plan.blocks] = total
+            for d in y_order:
+
+                @pl.when(lax.rem(yi + d, ny) // plan.blocks == i)
+                def _():
+                    y_copy(kind, d).start()
 
     def over_y(kind):
         total = ysum[kind, yi]
@@ -573,7 +574,8 @@
         for k, c in enumerate(order):
             core_copy(kind, c, k).wait_send()
         for to in steps[:-1]:
-            x_copy(kind, to).wait_send()
+            for i in range(span):
+                x_copy(kind, to, i).wait_send()
         for d in range(1, ny):
             y_copy(kind, d).wait_send()
 
@@ -611,7 +613,7 @@
         vm((plan.tm, plan.slots, L), F32), vm((plan.tm, plan.slots, L), F32),
         *[pltpu.SemaphoreType.REGULAR] * 3, dma((3,)),
         dma((gs,)), dma((gs,)), dma((gs,)), dma((gs,)), dma((ng, gs)), dma((ng,)),
-        dma((2, 8)), dma((2, 8)), dma((2, nx)), dma((2, nx)), dma((2, ny)), dma((2, ny)),
+        dma((2, 8)), dma((2, 8)), dma((2, 8)), dma((2, 8)), dma((2, ny)), dma((2, ny)),
         dma((plan.tm,)), dma((plan.tm,)),
     ]
     anywhere = pl.BlockSpec(memory_space=pl.ANY)

time: 42.8 us -> 42.7 us (level)
  the two profiles are of different devices: /device:TPU:1 before, /device:TPU:56 now
where the time goes in v5:
time: 42.7 us; the launch traced here: 42.5 us
  Pallas kernels  41.2 us (96%)
  local copies, waits for them, and re-layouts  0.67 us (2%)
  between operations  0.67 us (2%)
    pallas_call x1, Pallas kernels, on_device(): pl.pallas_call(functools.partial(kernel, plan), out_shape=shapes, in_spec...  40.5 us

profile of v5, /device:TPU:56, one launch (start us, length us, event | category | flops | bytes accessed | tf_op | source)
XLA Modules:
  0.0 42.5 jit_solution(5699744874986355961)
XLA Ops:
  0.6 0.0 copy-start
  0.6 0.0 copy-start.1
  0.7 0.0 copy-start.2
  0.7 0.7 %copy-done = f32[1024,1]{0,1:T(1,128)S(1)} copy-done((f32[1024,1]{0,1:T(1,128)S(1)}, f32[1024,1]{0,1:T(1,128)}, u32[]{:S(2)}) %copy-start) | copy-done | bytes 4120
  1.3 0.0 copy-done.1
  1.3 0.0 copy-done.2
  1.3 40.5 %shard_map.93 = (bf16[64,1024]{1,0:T(8,128)(2,1)S(1)}, f32[16,256]{1,0:T(8,128)S(1)}, f32[8,128]{1,0:T(8,128)S(1)}, f32[64,64]{1,0:T(8,128)S(1)}) custom-call(bf16[64,1024]{1,0:T(8,128)(2,1)} %bitcast.10, bf16[64,1024]{1,0:T(8,128)(2,1)} %bitcast.11, bf16[1024,256]{1,0:T(8,128)(2,1)} %bc_hbm.1, f32[8,128]{1,0:T(8,128)S(1)} %bitcast.7, s32[1,32]{1,0:T(1,128)S(1)} %bitcast.8, ...), custom_call_target="tpu_custom_call" | custom-call | tf_op jit(solution)/shard_map/pallas_call | solution.py:621
  41.8 0.7 %shard_map.94 = (bf16[64,1024]{1,0:T(8,128)(2,1)}, f32[16,256]{1,0:T(8,128)}, f32[8,128]{1,0:T(8,128)}, f32[64,64]{1,0:T(8,128)}) custom-call(bf16[64,1024]{1,0:T(8,128)(2,1)S(1)} %get-tuple-element.12.a, f32[16,256]{1,0:T(8,128)S(1)} %get-tuple-element.13.b, f32[8,128]{1,0:T(8,128)S(1)} %get-tuple-element.14.c, f32[64,64]{1,0:T(8,128)S(1)} %get-tuple-element.15.d), custom_call_target="tpu_custom_call" | custom-call | tf_op jit(solution)/shard_map/pallas_call | solution.py:633
Async XLA Ops:
  0.6 0.7 %copy-start = (f32[1024,1]{0,1:T(1,128)S(1)}, f32[1024,1]{0,1:T(1,128)}, u32[]{:S(2)}) copy-start(f32[1024,1]{0,1:T(1,128)} %param.8) | copy-start | bytes 12292
  0.6 0.7 %copy-start.1 = (s32[32,1]{0,1:T(1,128)S(1)}, s32[32,1]{0,1:T(1,128)}, u32[]{:S(2)}) copy-start(s32[32,1]{0,1:T(1,128)} %param.10) | copy-start | bytes 388
  0.7 0.7 %copy-start.2 = (s32[32,1]{0,1:T(1,128)S(1)}, s32[32,1]{0,1:T(1,128)}, u32[]{:S(2)}) copy-start(s32[32,1]{0,1:T(1,128)} %param.11) | copy-start | bytes 388
